TPU v7x, 256 devices: a whole 4x4x8 slice. The times are simulated.
256 devices in a mesh: ctx: 64 (over x, z, core), head: 4 (over y).
Axes of the slice: x: 4, y: 4, z: 8, core: 2. Of those that a mesh axis runs over, the one named last changes fastest.
Arguments:
- feat_in: bfloat16 [16384, 8192], P('ctx', 'head'), may hold values from -6 to 6
- gate_in: bfloat16 [16384, 8192], P('ctx', 'head'), may hold values from -6 to 6
- state_proj: bfloat16 [16384, 256], P('ctx'), may hold values from -1.5 to 1.5
- step_raw: float32 [64, 16384], P('head', 'ctx'), may hold values from -6 to 6
- doc_offset: int32 [16384], P('ctx'), may hold values from 0 to 4095, as said below
- feat_taps: float32 [4, 8192], P(None, 'head'), may hold values from -3 to 3
- feat_bias: float32 [8192], P('head'), may hold values from -1.5 to 1.5
- proj_taps: float32 [4, 256], replicated, may hold values from -3 to 3
- proj_bias: float32 [256], replicated, may hold values from -0.6 to 0.6
- step_bias: float32 [64], P('head'), may hold values from -4 to -1
- decay_log: float32 [64], P('head'), may hold values from -13 to -0.7
- skip_gain: float32 [64], P('head'), may hold values from 0.5 to 1.5
- norm_gain: float32 [8192], P('head'), may hold values from 0.1 to 1.9
Outputs:
- mixer_out: bfloat16 [16384, 8192], P('ctx', 'head')
Inputs may be any that keep to these rules, and one draw needn't show every extreme that they name: `doc_offset`: the position of each token within its document: 0 at a document's first token, rising by one per token inside it. A document holds at most 4096 tokens, and every document but the window's last holds more than 512.
All inputs are finite; a program needn't handle non-finite values.
Results may differ from a plain program's by a relative error of at most 0.006.
Values may be sent and summed in bfloat16 or wider, within the bound.
No kernel may reach another device: no remote copies, remote signals or barrier semaphores. Data moves between devices by JAX's collectives and lax.ppermute only.
A program may use at most 64 MiB of HBM per device.

v0:
```python
import jax
import jax.numpy as jnp
from jax import lax
from jax.sharding import PartitionSpec as P


def passed_along(block, axis, distance):
    devices = range(lax.axis_size(axis))
    route = [(i - distance, i) for i in devices if i - distance in devices]
    return lax.ppermute(block, axis, route)


def sent_to_all(array, axis):
    copies = jnp.broadcast_to(array, (lax.axis_size(axis), *array.shape))
    return lax.all_to_all(copies, axis, split_axis=0, concat_axis=0, tiled=True)


def of_everyone(array, axis):
    everything = sent_to_all(array, axis)
    return jnp.sum(everything, axis=0)


def causal_taps(values, rim_rows, kernel_taps, kernel_bias, offsets):
    row_count = values.shape[0]
    tap_count = kernel_taps.shape[0]
    joined = jnp.concatenate([rim_rows, values], axis=0).astype(jnp.float32)
    summed = jnp.broadcast_to(kernel_bias[None, :], values.shape)
    for tap_index in range(tap_count):
        tap_lag = tap_count - 1 - tap_index
        window_rows = lax.slice_in_dim(joined, tap_index, tap_index + row_count, axis=0)
        summed = summed + jnp.where(
            (offsets >= tap_lag)[:, None], kernel_taps[tap_index][None, :] * window_rows, 0.0
        )
    return jax.nn.silu(summed).astype(jnp.bfloat16)


def combine_states(earlier_part, later_part):
    return (
        earlier_part[0] * later_part[0],
        later_part[0][:, None, None] * earlier_part[1] + later_part[1],
    )


def body(
    feat_in,
    gate_in,
    state_proj,
    step_raw,
    doc_offset,
    feat_taps,
    feat_bias,
    proj_taps,
    proj_bias,
    step_bias,
    decay_log,
    skip_gain,
    norm_gain,
):
    head_count = step_raw.shape[0]
    row_count = feat_in.shape[0]
    head_dim = feat_in.shape[1] // head_count
    state_size = state_proj.shape[1] // 2
    tap_count = feat_taps.shape[0]
    rim_feat, rim_proj = passed_along(
        (feat_in[row_count - tap_count + 1 :], state_proj[row_count - tap_count + 1 :]), "ctx", 1
    )
    conv_feat = causal_taps(feat_in, rim_feat, feat_taps, feat_bias, doc_offset)
    conv_proj = causal_taps(state_proj, rim_proj, proj_taps, proj_bias, doc_offset)
    step_all = jax.nn.softplus(step_raw + step_bias[:, None])
    rate_all = step_all * (-jnp.exp(decay_log))[:, None]
    block_rows = min(512, row_count)
    position = jnp.arange(block_rows, dtype=jnp.int32)
    causal = position[None, :] <= position[:, None]
    final_row = block_rows - 1
    element_decay = jnp.ones((head_count,), jnp.float32)
    element_state = jnp.zeros((head_count, head_dim, state_size), jnp.float32)
    block_index = 0
    start = block_index * block_rows
    feat_block = conv_feat.reshape(block_rows, head_count, head_dim)
    in_block = conv_proj[start : start + block_rows, :state_size]
    out_block = conv_proj[start : start + block_rows, state_size:]
    cumulative = jnp.cumsum(rate_all, axis=1)
    same_doc = causal & (doc_offset[:, None] >= position[:, None] - position[None, :])
    scores = jnp.dot(out_block, in_block.T, preferred_element_type=jnp.float32)
    exponent_gap = jnp.where(
        same_doc[None], cumulative[:, :, None] - cumulative[:, None, :], -jnp.inf
    )
    weights = (scores[None] * jnp.exp(exponent_gap) * step_all[:, None, :]).astype(jnp.bfloat16)
    inner_out = jnp.einsum("hts,shp->thp", weights, feat_block, preferred_element_type=jnp.float32)
    reaches = doc_offset >= position + 1
    tail_mask = doc_offset[final_row] >= final_row - position
    tail_coef = jnp.where(
        tail_mask[None, :],
        jnp.exp(cumulative[:, final_row : final_row + 1] - cumulative) * step_all,
        0.0,
    )
    scaled = (in_block.astype(jnp.float32)[None] * tail_coef[:, :, None]).astype(jnp.bfloat16)
    contrib = jnp.einsum("shp,hsn->hpn", feat_block, scaled, preferred_element_type=jnp.float32)
    keep_factor = jnp.where(reaches[final_row], jnp.exp(cumulative[:, final_row]), 0.0)
    saved_blocks = [(feat_block, out_block, cumulative, reaches, inner_out, contrib, keep_factor)]
    element_state = keep_factor[:, None, None] * element_state + contrib
    element_decay = element_decay * keep_factor
    longest_doc = row_count * lax.axis_size("ctx") // 4
    span_back = (longest_doc + row_count - 2) // row_count
    distances = [1]
    window_size = 1
    while window_size < span_back:
        distances.append(window_size)
        window_size = window_size * 2
    current = (element_decay, element_state)
    for turn_index, distance in enumerate(distances):
        moved = passed_along((current[0], current[1]), "ctx", distance)
        if turn_index == 0:
            current = moved
        else:
            current = combine_states(moved, current)
    start_state = current[1]
    pieces_out = []
    for block_index, saved in enumerate(saved_blocks):
        feat_block, out_block, cumulative, reaches, inner_out, contrib, keep_factor = saved
        lift_factor = jnp.where(reaches[None, :], jnp.exp(cumulative), 0.0)
        from_state = (
            jnp.einsum(
                "tn,hpn->thp",
                out_block.astype(jnp.float32),
                start_state,
                precision=lax.Precision.HIGHEST,
            )
            * lift_factor.T[:, :, None]
        )
        pieces_out.append(
            inner_out + from_state + skip_gain[None, :, None] * feat_block.astype(jnp.float32)
        )
    mixed = pieces_out[0].reshape(row_count, head_count * head_dim)
    gated = mixed * jax.nn.silu(gate_in.astype(jnp.float32))
    squares = jnp.sum(gated * gated, axis=1)
    total_squares = of_everyone(squares, "head")
    scale = lax.rsqrt(total_squares / (head_count * head_dim * lax.axis_size("head")) + 1e-05)
    return (gated * scale[:, None] * norm_gain[None, :]).astype(jnp.bfloat16)


def solution(mesh):
    return jax.shard_map(
        body,
        mesh=mesh,
        in_specs=(
            P("ctx", "head"),
            P("ctx", "head"),
            P("ctx", None),
            P("head", "ctx"),
            P("ctx"),
            P(None, "head"),
            P("head"),
            P(),
            P(),
            P("head"),
            P("head"),
            P("head"),
            P("head"),
        ),
        out_specs=P("ctx", "head"),
        check_vma=False,
    )
```

profile of v0, /device:TPU:6, one launch (start us, length us, event | category | flops | bytes accessed | tf_op | source)
XLA Modules:
  0.0 204.3 jit_solution(13575930539501242746)
XLA Ops:
  0.8 1.9 collective-permute-start.1
  3.5 3.9 %collective-permute-start = (bf16[3,2048]{1,0:T(4,128)(2,1)S(1)}, bf16[3,2048]{1,0:T(4,128)(2,1)S(1)}, u32[]{:S(2)}, u32[]{:S(2)}) collective-permute-start(bf16[3,2048]{1,0:T(4,128)(2,1)S(1)} %slice.77), channel_id=1, source_target_pairs={{0,4},{4,8},{8,12},{12,16},{16,20},{20,24},{24,28},{28,32},{32,36}... | collective-permute-start | bytes 36872 | tf_op jit(solution)/shard_map/ppermute | solution.py:10
  7.4 1.3 slice.100
  17.9 2.3 %multiply_convert_fusion.4 = bf16[256,2048]{1,0:T(8,128)(2,1)S(1)} fusion(f32[259,2048]{1,0:T(8,128)S(1)} %maximum_convert_fusion, f32[2048]{0:T(1024)S(1)} %bitcast.45, f32[2048]{0:T(1024)S(1)} %bitcast.46, f32[2048]{0:T(1024)S(1)} %bitcast.44, f32[2048]{0:T(1024)S(1)} %bitcast.43, f32[2048]{0:T(1024)S(1)} %copy-done.2, ...), kind=kLoop, calls=%fused_computation.30 | loop fusion | flops 8912896 | bytes 9479168 | tf_op jit(solution)/shard_map/convert_element_type | solution.py:34
  21.6 1.9 collective-permute-start.6
  23.6 16.3 %collective-permute-done.6 = f32[16,128,128]{2,1,0:T(8,128)S(1)} collective-permute-done((f32[16,128,128]{2,1,0:T(8,128)S(1)}, f32[16,128,128]{2,1,0:T(8,128)S(1)}, u32[]{:S(2)}, u32[]{:S(2)}) %collective-permute-start.6) | collective-permute-done | bytes 1048608 | tf_op jit(solution)/shard_map/ppermute | solution.py:10
  39.9 1.9 collective-permute-start.7
  41.8 1.9 collective-permute-start.2
  43.7 14.4 %collective-permute-done.2 = f32[16]{0:T(128)S(1)} collective-permute-done((f32[16]{0:T(128)S(1)}, f32[16]{0:T(128)S(1)}, u32[]{:S(2)}, u32[]{:S(2)}) %collective-permute-start.2) | collective-permute-done | bytes 96 | tf_op jit(solution)/shard_map/ppermute | solution.py:10
  58.3 1.9 collective-permute-start.8
  60.2 1.9 collective-permute-start.3
  62.2 15.7 %collective-permute-done.3 = f32[16]{0:T(128)S(1)} collective-permute-done((f32[16]{0:T(128)S(1)}, f32[16]{0:T(128)S(1)}, u32[]{:S(2)}, u32[]{:S(2)}) %collective-permute-start.3) | collective-permute-done | bytes 96 | tf_op jit(solution)/shard_map/ppermute | solution.py:10
  77.9 5.3 %collective-permute-done.8 = f32[16,128,128]{2,1,0:T(8,128)S(1)} collective-permute-done((f32[16,128,128]{2,1,0:T(8,128)S(1)}, f32[16,128,128]{2,1,0:T(8,128)S(1)}, u32[]{:S(2)}, u32[]{:S(2)}) %collective-permute-start.8) | collective-permute-done | bytes 1048608 | tf_op jit(solution)/shard_map/ppermute | solution.py:10
  83.4 3.8 %collective-permute-start.9 = (f32[16,128,128]{2,1,0:T(8,128)S(1)}, f32[16,128,128]{2,1,0:T(8,128)S(1)}, u32[]{:S(2)}, u32[]{:S(2)}) collective-permute-start(f32[16,128,128]{2,1,0:T(8,128)S(1)} %multiply_add_fusion.1), channel_id=1, source_target_pairs={{0,16},{4,20},{8,24},{12,28},{16,32},{20,36},{24,40},{28,44},{32,4... | collective-permute-start | bytes 3145736 | tf_op jit(solution)/shard_map/ppermute | solution.py:10
  87.2 4.1 %collective-permute-start.4 = (f32[16]{0:T(128)S(1)}, f32[16]{0:T(128)S(1)}, u32[]{:S(2)}, u32[]{:S(2)}) collective-permute-start(f32[16]{0:T(128)S(1)} %mul.251), channel_id=1, source_target_pairs={{0,8},{4,12},{8,16},{12,20},{16,24},{20,28},{24,32},{28,36},{32,40... | collective-permute-start | bytes 200 | tf_op jit(solution)/shard_map/ppermute | solution.py:10
  91.3 39.4 %collective-permute-done.4 = f32[16]{0:T(128)S(1)} collective-permute-done((f32[16]{0:T(128)S(1)}, f32[16]{0:T(128)S(1)}, u32[]{:S(2)}, u32[]{:S(2)}) %collective-permute-start.4) | collective-permute-done | bytes 96 | tf_op jit(solution)/shard_map/ppermute | solution.py:10
  130.9 7.4 %collective-permute-start.10 = (f32[16,128,128]{2,1,0:T(8,128)S(1)}, f32[16,128,128]{2,1,0:T(8,128)S(1)}, u32[]{:S(2)}, u32[]{:S(2)}) collective-permute-start(f32[16,128,128]{2,1,0:T(8,128)S(1)} %multiply_add_fusion), channel_id=1, source_target_pairs={{0,32},{4,36},{8,40},{12,44},{16,48},{20,52},{24,56},{28,60},{32,6... | collective-permute-start | bytes 3145736 | tf_op jit(solution)/shard_map/ppermute | solution.py:10
  138.3 1.9 collective-permute-start.5
  140.4 45.6 %collective-permute-done.5 = f32[16]{0:T(128)S(1)} collective-permute-done((f32[16]{0:T(128)S(1)}, f32[16]{0:T(128)S(1)}, u32[]{:S(2)}, u32[]{:S(2)}) %collective-permute-start.5) | collective-permute-done | bytes 96 | tf_op jit(solution)/shard_map/ppermute | solution.py:10
  186.2 1.3 fusion
  187.5 2.5 %fusion.13 = f32[256,16,128]{0,2,1:T(8,128)} fusion(f32[16,128,256]{2,1,0:T(8,128)S(1)} %fusion, bf16[256,16,128]{0,2,1:T(8,128)(2,1)S(1)} %bitcast.41, f32[16]{0:T(128)S(1)} %copy-done.5, f32[256,16]{0,1:T(8,128)S(1)} %get-tuple-element.14, f32[16,128,128]{2,1,0:T(8,128)S(1)} %multiply_add_fusion, f32[16,128,128]{2,1,0:T(8,128)S(1)} %collective-permute-done.10, ...), kind=kOutput, calls=%fused_computation.21 | convolution fusion | flops 808452096 | bytes 7422976 | tf_op jit(solution)/shard_map/tn,hpn->thp/dot_general | solution.py:123
  190.0 2.0 copy.28
  192.8 9.6 %all_to_all.6 = f32[4,1,256]{2,1,0:T(1,128)S(1)} all-to-all(f32[4,1,256]{2,1,0:T(1,128)S(1)} %broadcast_in_dim.158), channel_id=1, replica_groups=mesh['ctx'=64,'head'=4] {'head'}, dimensions={0} | all-to-all | bytes 8192 | tf_op jit(solution)/shard_map/all_to_all | solution.py:15
  202.4 1.8 multiply_convert_fusion.2
  (53 shorter events, 13.7 us)
Async XLA Ops:
  0.0 17.6 %copy-start.1 = (bf16[256,2048]{1,0:T(8,128)(2,1)S(1)}, bf16[256,2048]{1,0:T(8,128)(2,1)}, u32[]{:S(2)}) copy-start(bf16[256,2048]{1,0:T(8,128)(2,1)} %param.13) | copy-start | bytes 3145732
  0.8 14.9 %collective-permute-start.1 = (bf16[3,256]{1,0:T(4,128)(2,1)S(1)}, bf16[3,256]{1,0:T(4,128)(2,1)S(1)}, u32[]{:S(2)}, u32[]{:S(2)}) collective-permute-start(bf16[3,256]{1,0:T(4,128)(2,1)S(1)} %slice.86), channel_id=1, source_target_pairs={{0,4},{4,8},{8,12},{12,16},{16,20},{20,24},{24,28},{28,32},{32,36}... | collective-permute-start | bytes 4616 | tf_op jit(solution)/shard_map/ppermute | solution.py:10
  3.5 14.1 %collective-permute-start = (bf16[3,2048]{1,0:T(4,128)(2,1)S(1)}, bf16[3,2048]{1,0:T(4,128)(2,1)S(1)}, u32[]{:S(2)}, u32[]{:S(2)}) collective-permute-start(bf16[3,2048]{1,0:T(4,128)(2,1)S(1)} %slice.77), channel_id=1, source_target_pairs={{0,4},{4,8},{8,12},{12,16},{16,20},{20,24},{24,28},{28,32},{32,36}... | collective-permute-start | bytes 36872 | tf_op jit(solution)/shard_map/ppermute | solution.py:10
  16.6 1.3 copy-start.2
  21.6 18.2 %collective-permute-start.6 = (f32[16,128,128]{2,1,0:T(8,128)S(1)}, f32[16,128,128]{2,1,0:T(8,128)S(1)}, u32[]{:S(2)}, u32[]{:S(2)}) collective-permute-start(f32[16,128,128]{2,1,0:T(8,128)S(1)} %convolution_add_fusion), channel_id=1, source_target_pairs={{0,4},{4,8},{8,12},{12,16},{16,20},{20,24},{24,28},{28,32},{32,36}... | collective-permute-start | bytes 3145736 | tf_op jit(solution)/shard_map/ppermute | solution.py:10
  39.9 18.3 %collective-permute-start.7 = (f32[16,128,128]{2,1,0:T(8,128)S(1)}, f32[16,128,128]{2,1,0:T(8,128)S(1)}, u32[]{:S(2)}, u32[]{:S(2)}) collective-permute-start(f32[16,128,128]{2,1,0:T(8,128)S(1)} %collective-permute-done.6), channel_id=1, source_target_pairs={{0,4},{4,8},{8,12},{12,16},{16,20},{20,24},{24,28},{28,32},{32,36}... | collective-permute-start | bytes 3145736 | tf_op jit(solution)/shard_map/ppermute | solution.py:10
  41.8 16.4 %collective-permute-start.2 = (f32[16]{0:T(128)S(1)}, f32[16]{0:T(128)S(1)}, u32[]{:S(2)}, u32[]{:S(2)}) collective-permute-start(f32[16]{0:T(128)S(1)} %get-tuple-element.6), channel_id=1, source_target_pairs={{0,4},{4,8},{8,12},{12,16},{16,20},{20,24},{24,28},{28,32},{32,36}... | collective-permute-start | bytes 200 | tf_op jit(solution)/shard_map/ppermute | solution.py:10
  58.3 24.9 %collective-permute-start.8 = (f32[16,128,128]{2,1,0:T(8,128)S(1)}, f32[16,128,128]{2,1,0:T(8,128)S(1)}, u32[]{:S(2)}, u32[]{:S(2)}) collective-permute-start(f32[16,128,128]{2,1,0:T(8,128)S(1)} %multiply_add_fusion.2), channel_id=1, source_target_pairs={{0,8},{4,12},{8,16},{12,20},{16,24},{20,28},{24,32},{28,36},{32,40... | collective-permute-start | bytes 3145736 | tf_op jit(solution)/shard_map/ppermute | solution.py:10
  60.2 17.7 %collective-permute-start.3 = (f32[16]{0:T(128)S(1)}, f32[16]{0:T(128)S(1)}, u32[]{:S(2)}, u32[]{:S(2)}) collective-permute-start(f32[16]{0:T(128)S(1)} %collective-permute-done.2), channel_id=1, source_target_pairs={{0,4},{4,8},{8,12},{12,16},{16,20},{20,24},{24,28},{28,32},{32,36}... | collective-permute-start | bytes 200 | tf_op jit(solution)/shard_map/ppermute | solution.py:10
  83.3 56.9 %copy-start.4 = (s32[256]{0:T(256)S(1)}, s32[256]{0:T(256)}, u32[]{:S(2)}) copy-start(s32[256]{0:T(256)} %param.17) | copy-start | bytes 3076
  83.4 47.4 %collective-permute-start.9 = (f32[16,128,128]{2,1,0:T(8,128)S(1)}, f32[16,128,128]{2,1,0:T(8,128)S(1)}, u32[]{:S(2)}, u32[]{:S(2)}) collective-permute-start(f32[16,128,128]{2,1,0:T(8,128)S(1)} %multiply_add_fusion.1), channel_id=1, source_target_pairs={{0,16},{4,20},{8,24},{12,28},{16,32},{20,36},{24,40},{28,44},{32,4... | collective-permute-start | bytes 3145736 | tf_op jit(solution)/shard_map/ppermute | solution.py:10
  87.2 43.6 %collective-permute-start.4 = (f32[16]{0:T(128)S(1)}, f32[16]{0:T(128)S(1)}, u32[]{:S(2)}, u32[]{:S(2)}) collective-permute-start(f32[16]{0:T(128)S(1)} %mul.251), channel_id=1, source_target_pairs={{0,8},{4,12},{8,16},{12,20},{16,24},{20,28},{24,32},{28,36},{32,40... | collective-permute-start | bytes 200 | tf_op jit(solution)/shard_map/ppermute | solution.py:10
  130.9 56.6 %collective-permute-start.10 = (f32[16,128,128]{2,1,0:T(8,128)S(1)}, f32[16,128,128]{2,1,0:T(8,128)S(1)}, u32[]{:S(2)}, u32[]{:S(2)}) collective-permute-start(f32[16,128,128]{2,1,0:T(8,128)S(1)} %multiply_add_fusion), channel_id=1, source_target_pairs={{0,32},{4,36},{8,40},{12,44},{16,48},{20,52},{24,56},{28,60},{32,6... | collective-permute-start | bytes 3145736 | tf_op jit(solution)/shard_map/ppermute | solution.py:10
  138.3 47.7 %collective-permute-start.5 = (f32[16]{0:T(128)S(1)}, f32[16]{0:T(128)S(1)}, u32[]{:S(2)}, u32[]{:S(2)}) collective-permute-start(f32[16]{0:T(128)S(1)} %mul.252), channel_id=1, source_target_pairs={{0,16},{4,20},{8,24},{12,28},{16,32},{20,36},{24,40},{28,44},{32,4... | collective-permute-start | bytes 200 | tf_op jit(solution)/shard_map/ppermute | solution.py:10
  186.2 1.4 copy-start.5
  190.0 2.0 copy-start
  192.1 10.4 %copy-start.3 = (f32[2048]{0:T(1024)S(1)}, f32[2048]{0:T(1024)}, u32[]{:S(2)}) copy-start(f32[2048]{0:T(1024)} %param.25) | copy-start | bytes 24580
where the time goes:
time: 205 us; the launch traced here: 204 us
  waiting for transfers between devices  137 us (67%)
  starting transfers between devices  32.7 us (16%)
  other arithmetic  11.9 us (6%)
  blocking collectives  9.55 us (5%)
  local copies, waits for them, and re-layouts  8.11 us (4%)
  matrix products  4.84 us (2%)
    ppermute x11, waiting for transfers between devices, passed_along(): return lax.ppermute(block, axis, route)  137 us
    ppermute x11, starting transfers between devices, passed_along(): return lax.ppermute(block, axis, route)  32.7 us
    all_to_all x1, blocking collectives, sent_to_all(): return lax.all_to_all(copies, axis, split_axis=0, concat_axis=0, tiled=True)  9.55 us
  transfers between devices with their start and end apart: 11, of which 6 were waited for; matrix products, arithmetic and copies ran while one was open for 6% of the time, Pallas kernels for 0%

commit v1 on v0

v1 whole, which is shorter than its diff:
```python
import functools

import jax
import jax.numpy as jnp
from jax import lax
from jax.experimental import pallas as pl
from jax.experimental.pallas import tpu as pltpu
from jax.sharding import PartitionSpec as P

F32 = jnp.float32
BF16 = jnp.bfloat16
ROWS = 256
HEADS = 16
HALF = 8
HD = 128
COLS = HEADS * HD
TAPS = 4
XS, ZS, CS, YS = 4, 8, 2, 4
LOG2E = 1.4426950408889634
VMEM_LIMIT = 40 * 1024 * 1024


def spots():
    return [(x, z, c) for x in range(XS) for z in range(ZS) for c in range(CS)]


def place(x, z, c):
    return (x * ZS + z) * CS + c


def route(to):
    pairs = []
    for x, z, c in spots():
        target = to(x, z, c)
        if target is not None:
            pairs.append((place(x, z, c), place(*target)))
    return pairs


NEXT = [(i, i + 1) for i in range(XS * ZS * CS - 1)]
CORE = route(lambda x, z, c: (x, z, 1 - c))


APART = route(lambda x, z, c: (x, z ^ (1 + 2 * c), c))
TWO = route(lambda x, z, c: (x, z ^ 2, c))


def to_later_group(x, z, c):
    if c == 0 and z < 4:
        return (x, z ^ 6, c)
    if x + 1 == XS:
        return None
    return (x + 1, z ^ 6 if c == 0 else z, c)


LATER = route(to_later_group)
HEAD_XOR = {m: [(i, i ^ m) for i in range(YS)] for m in (1, 2, 3)}


def my_core():
    return lax.rem(lax.axis_index("ctx"), 2)


def my_spot():
    return lax.rem(lax.div(lax.axis_index("ctx"), 2), 4)


def my_slice():
    z = lax.rem(lax.div(lax.axis_index("ctx"), 2), ZS)
    spot = lax.rem(z, 4)
    return jnp.where(z >= 4, lax.bitwise_xor(spot, 2), spot)


def silu(v):
    half = 0.5 * v
    return half + half * jnp.tanh(half)


def conv_rows(xs, taps_ref, bias_ref, cols, scratch_cols, base, rows, masks):
    acc = jnp.broadcast_to(bias_ref[0:1, cols], (rows, HD))
    for k in range(TAPS):
        lag = TAPS - 1 - k
        window = xs[base - lag : base - lag + rows, scratch_cols]
        if lag:
            window = jnp.where(masks[lag], window, 0.0)
        acc = acc + taps_ref[k : k + 1, cols] * window
    return silu(acc).astype(BF16)


PACK = 640
PACKS = [(j, min(PACK, COLS + 256 - j)) for j in range(0, COLS + 256, PACK)]


def edge_kernel(
    doc_hbm, feat_hbm, proj_hbm, ftaps_hbm, fbias_hbm, ptaps_hbm, pbias_hbm, raw_hbm,
    out_ref, docv_ref, feat_ref, proj_ref, ftaps_ref, fbias_ref, ptaps_ref, pbias_ref, raw_ref,
    doc_ref, sems,
):
    copies = [
        pltpu.make_async_copy(source, target, sems.at[n])
        for n, (source, target) in enumerate((
            (feat_hbm, feat_ref), (proj_hbm, proj_ref), (doc_hbm, doc_ref),
            (ftaps_hbm, ftaps_ref), (fbias_hbm, fbias_ref), (ptaps_hbm, ptaps_ref),
            (pbias_hbm, pbias_ref), (raw_hbm, raw_ref),
        ))
    ]
    for copy in copies:
        copy.start()
    for copy in copies[:2]:
        copy.wait()
    last = jnp.concatenate(
        [feat_ref[ROWS - 16 :, :].astype(F32), proj_ref[ROWS - 16 :, :].astype(F32)], axis=1
    )
    last = last[16 - (TAPS - 1) :]
    rows = []
    for j, width in PACKS:
        piece = last[:, j : j + width]
        if width < PACK:
            piece = jnp.concatenate([piece, jnp.zeros((TAPS - 1, PACK - width), F32)], axis=1)
        rows.append(piece)
    rows.append(jnp.zeros((16 - (TAPS - 1) * len(PACKS), PACK), F32))
    out_ref[...] = jnp.concatenate(rows, axis=0).astype(BF16)
    for copy in copies[2:]:
        copy.wait()
    row = lax.broadcasted_iota(jnp.int32, (8, HD), 0)
    docv_ref[...] = jnp.where(row == 0, doc_ref[0], (ROWS - 1) - doc_ref[ROWS - 1])


def split_decay(value):
    high = jnp.floor(value * 256.0) * (1.0 / 256.0)
    return jnp.concatenate([high, value - high], axis=0).astype(BF16)


def joined_decay(tile):
    wide = tile.astype(F32)
    half = tile.shape[0] // 2
    return wide[:half] + wide[half:]


def conv_kernel(
    docv_ref, feat_ref, proj_ref, ftaps_ref, fbias_ref, ptaps_ref, pbias_ref, raw_ref,
    sbias_hbm, dlog_hbm,
    featc_ref, projc_ref, cum_ref, step_ref, coef_ref, decay_ref, sbias_ref, dlog_ref, sems,
):
    copies = [
        pltpu.make_async_copy(sbias_hbm, sbias_ref, sems.at[0]),
        pltpu.make_async_copy(dlog_hbm, dlog_ref, sems.at[1]),
    ]
    for copy in copies:
        copy.start()
    first, start = docv_ref[0:1], docv_ref[1:2]
    first = jnp.concatenate([first, first], axis=1)
    start = jnp.concatenate([start, start], axis=1)
    t = lax.broadcasted_iota(jnp.int32, (ROWS, ROWS), 0)
    s = lax.broadcasted_iota(jnp.int32, (ROWS, ROWS), 1)
    offs = jnp.where((start > 0) & (t >= start), t - start, first + t)
    shifts = [
        jnp.where((t - s == lag) & (offs >= lag), 1.0, 0.0).astype(BF16) for lag in (1, 2, 3)
    ]

    def conv(x_ref, taps_ref, bias_ref, out_ref):
        for j in range(0, out_ref.shape[1], 256):
            cols = slice(j, j + 256)
            x = x_ref[:, cols]
            acc = jnp.broadcast_to(bias_ref[0:1, cols], (ROWS, 256))
            for k in range(TAPS):
                lag = TAPS - 1 - k
                if lag:
                    moved = jnp.dot(shifts[lag - 1], x, preferred_element_type=F32)
                else:
                    moved = x.astype(F32)
                acc = acc + taps_ref[k : k + 1, cols] * moved
            out_ref[:, cols] = silu(acc).astype(BF16)

    conv(proj_ref, ptaps_ref, pbias_ref, projc_ref)
    conv(feat_ref, ftaps_ref, fbias_ref, featc_ref)

    for copy in copies:
        copy.wait()
    first, start = first[:, 0:1], start[:, 0:1]
    line = lax.broadcasted_iota(jnp.int32, (HEADS, ROWS), 0)
    lane = lax.broadcasted_iota(jnp.int32, (HEADS, ROWS), 1)
    bias = jnp.zeros((HEADS, ROWS), F32)
    speed = jnp.zeros((HEADS, ROWS), F32)
    for h in range(HEADS):
        bias = jnp.where(line == h, sbias_ref[h], bias)
        speed = jnp.where(line == h, dlog_ref[h], speed)
    v = raw_ref[...] + bias
    step = jnp.maximum(v, 0.0) + jnp.log1p(jnp.exp(-jnp.abs(v)))
    cum = -step * jnp.exp(speed)
    shift = 1
    while shift < ROWS:
        cum = cum + jnp.where(lane >= shift, pltpu.roll(cum, shift, 1), 0.0)
        shift *= 2
    last = cum[:, ROWS - 1 : ROWS]
    cum_ref[...] = cum
    step_ref[...] = step
    tail = (start <= 0) | (lane >= start)
    coef_ref[...] = jnp.where(tail, jnp.exp(last - cum) * step, 0.0)
    kept = (docv_ref[1:2] < 0) & (docv_ref[0:1] >= 1)
    decay_ref[...] = jnp.where(kept, jnp.broadcast_to(jnp.exp(last), (HEADS, HD)), 0.0)


def state_kernel(
    docv_ref, rim_ref, feat_ref, proj_ref, ftaps_ref, fbias_ref, ptaps_ref, pbias_ref,
    coef_ref, decay_ref, featc_in, projc_in,
    featc_ref, projc_ref, keep_ref, send_ref, xs,
):
    del featc_in, projc_in
    rim = rim_ref[...].astype(F32)
    for n, (j, width) in enumerate(PACKS):
        xs[16 - (TAPS - 1) : 16, j : j + width] = rim[
            n * (TAPS - 1) : (n + 1) * (TAPS - 1), :width
        ]
    xs[16:32, :COLS] = feat_ref[0:16, :].astype(F32)
    xs[16:32, COLS:] = proj_ref[0:16, :].astype(F32)
    first, start = docv_ref[0:1], docv_ref[1:2]
    t = lax.broadcasted_iota(jnp.int32, (16, HD), 0)
    offs = jnp.where((start > 0) & (t >= start), t - start, first + t)
    masks = {lag: offs >= lag for lag in (1, 2, 3)}
    for j in range(2):
        cols = slice(j * HD, (j + 1) * HD)
        there = slice(COLS + j * HD, COLS + (j + 1) * HD)
        projc_ref[0:16, cols] = conv_rows(xs, ptaps_ref, pbias_ref, cols, there, 16, 16, masks)
    for j in range(HEADS):
        cols = slice(j * HD, (j + 1) * HD)
        featc_ref[0:16, cols] = conv_rows(xs, ftaps_ref, fbias_ref, cols, cols, 16, 16, masks)
    turned = projc_ref[:, :HD].astype(F32).T
    for h in range(HEADS):
        rows = slice(h * HD, (h + 1) * HD)
        scaled = (turned * coef_ref[h : h + 1, :]).astype(BF16)
        added = jnp.dot(scaled, featc_ref[:, rows], preferred_element_type=F32)
        keep_ref[rows, :] = added
        send_ref[rows, :] = added.astype(BF16)
    send_ref[COLS:, :] = split_decay(decay_ref[...])


def chip_kernel(keep_ref, decay_ref, recv_ref, own_ref, own_decay_ref, a_ref, b_ref, decays):
    core = my_core()
    second = core == 1
    k = my_slice()
    theirs = joined_decay(recv_ref[COLS:, :])
    mine = decay_ref[...]
    decays[0:16, :] = jnp.where(second, mine, theirs)
    decays[16:32, :] = mine * theirs
    decays[32:40, :] = jnp.zeros((8, HD), F32)

    def combined(h):
        rows = pl.ds(pl.multiple_of(h * HD, HD), HD)
        a = keep_ref[rows, :]
        b = recv_ref[rows, :].astype(F32)
        return decays[pl.ds(h, 1), :] * jnp.where(second, b, a) + jnp.where(second, a, b)

    s = lax.bitwise_xor(k, 1 + 2 * core)
    for i in range(4):
        a_ref[i * HD : (i + 1) * HD, :] = combined(4 * s + i).astype(BF16)
    a_ref[4 * HD :, :] = split_decay(decays[pl.ds(16 + 4 * s, 8), :])
    s = lax.bitwise_xor(k, 2)
    for i in range(2):
        b_ref[i * HD : (i + 1) * HD, :] = combined(4 * s + 2 * core + i).astype(BF16)
    b_ref[2 * HD :, :] = split_decay(decays[pl.ds(16 + 4 * s, 8), :])
    for i in range(4):
        own_ref[i * HD : (i + 1) * HD, :] = combined(4 * k + i)
    own_decay_ref[...] = decays[pl.ds(16 + 4 * k, 8), :]


QUARTER = 4 * HD


def half_rows(core):
    return pl.ds(pl.multiple_of(core * 2 * HD, 2 * HD), 2 * HD)


def group_kernel(
    own_ref, own_decay_ref, ra_ref, ga_ref, rb_ref, gb_ref,
    total_ref, chips_ref, decays_ref,
):
    core = my_core()
    spot = my_spot()
    chips_ref[spot] = own_ref[...]
    decays_ref[spot] = own_decay_ref[...]
    for ref, m in ((ra_ref, 1 + 2 * core), (ga_ref, 3 - 2 * core)):
        there = lax.bitwise_xor(spot, m)
        chips_ref[there] = ref[:QUARTER, :].astype(F32)
        decays_ref[there] = joined_decay(ref[QUARTER:, :])
    there = lax.bitwise_xor(spot, 2)
    chips_ref[there, half_rows(core), :] = rb_ref[: 2 * HD, :].astype(F32)
    chips_ref[there, half_rows(1 - core), :] = gb_ref[: 2 * HD, :].astype(F32)
    decays_ref[there] = joined_decay(rb_ref[2 * HD :, :])
    for i in range(4):
        rows = slice(i * HD, (i + 1) * HD)
        total = chips_ref[0, rows, :]
        for q in range(1, 4):
            total = decays_ref[q, i : i + 1, :] * total + chips_ref[q, rows, :]
        total_ref[rows, :] = total.astype(BF16)
    total_ref[QUARTER:, :] = split_decay(
        decays_ref[0] * decays_ref[1] * decays_ref[2] * decays_ref[3]
    )


def enter_kernel(chips_ref, decays_ref, q_ref, other_ref, own_ref, a_ref, b_ref, states):
    core = my_core()
    second = core == 1
    spot = my_spot()
    q = q_ref[...].astype(F32)
    other = other_ref[...].astype(F32)
    before = jnp.where(second, other, q)
    farther = jnp.where(second, q, other)
    decay = joined_decay(before[QUARTER:])
    for i in range(4):
        rows = slice(i * HD, (i + 1) * HD)
        state = before[rows] + decay[i : i + 1] * farther[rows]
        for n in range(4):
            states[n, rows, :] = state
            if n < 3:
                state = decays_ref[n, i : i + 1, :] * state + chips_ref[n, rows, :]
    a_ref[...] = states[lax.bitwise_xor(spot, 1 + 2 * core)].astype(BF16)
    b_ref[...] = states[lax.bitwise_xor(spot, 2), half_rows(core), :].astype(BF16)
    own_ref[...] = states[spot]


def inner_kernel(
    docv_ref, featc_ref, projc_ref, cum_ref, step_ref, gate_hbm, skip_hbm, gain_hbm,
    a_ref, g_ref, gain_ref, masked, gate_ref, skip_ref, sems,
):
    copies = [
        pltpu.make_async_copy(gate_hbm, gate_ref, sems.at[0]),
        pltpu.make_async_copy(skip_hbm, skip_ref, sems.at[1]),
        pltpu.make_async_copy(gain_hbm, gain_ref, sems.at[2]),
    ]
    for copy in copies:
        copy.start()
    first, start = docv_ref[0:1], docv_ref[1:2]
    scores = lax.dot_general(
        projc_ref[:, HD:], projc_ref[:, :HD], (((1,), (1,)), ((), ())),
        preferred_element_type=F32,
    )
    t = lax.broadcasted_iota(jnp.int32, (ROWS, ROWS), 0)
    s = lax.broadcasted_iota(jnp.int32, (ROWS, ROWS), 1)
    wide_start = jnp.concatenate([start, start], axis=1)
    same = (s <= t) & ((s >= wide_start) | (t < wide_start))
    masked[...] = jnp.where(same, scores, 0.0)
    cum = cum_ref[...] * LOG2E
    row_side = cum - jnp.log(step_ref[...]) * LOG2E
    padded = jnp.concatenate([cum, jnp.zeros((HD - HEADS, ROWS), F32)], axis=0)
    columns = padded.T
    t_col = lax.broadcasted_iota(jnp.int32, (ROWS, HD), 0)
    reach = (first >= 1) & ((t_col < start) | (start <= 0))
    for copy in copies:
        copy.wait()
    for h in range(HEADS):
        cols = slice(h * HD, (h + 1) * HD)
        column = jnp.broadcast_to(columns[:, h : h + 1], (ROWS, HD))
        lift = jnp.where(reach, jnp.exp2(column), 0.0)
        gate = silu(gate_ref[:, cols].astype(F32))
        g_ref[h] = gate * lift
        for top in (0, HD):
            width = top + HD
            tall = column[top : top + HD]
            wide = jnp.concatenate([tall] * (width // HD), axis=1)
            gap = jnp.minimum(wide - row_side[h : h + 1, :width], 60.0)
            weights = (masked[top : top + HD, :width] * jnp.exp2(gap)).astype(BF16)
            inner = jnp.dot(weights, featc_ref[:width, cols], preferred_element_type=F32)
            feat = featc_ref[top : top + HD, cols].astype(F32)
            a_ref[h, top : top + HD, :] = (inner + skip_ref[h] * feat) * gate[top : top + HD]


def lifted_heads(groups, second, decays, recv_ref, c, a_ref, g_ref, total, keep):
    for ref, base, count in groups:
        for i in range(count):
            h = base + i
            rows = pl.ds(pl.multiple_of(h * HD, HD), HD)
            state = ref[i * HD : (i + 1) * HD, :].astype(F32)
            middle = decays[pl.ds(h, 1), :] * state + recv_ref[rows, :].astype(F32)
            state = jnp.where(second, middle, state)
            high = state.astype(BF16)
            low = (state - high.astype(F32)).astype(BF16)
            lifted = jnp.dot(c, high, preferred_element_type=F32) + jnp.dot(
                c, low, preferred_element_type=F32
            )
            gated = a_ref[h] + lifted * g_ref[h]
            keep(h, gated)
            total = total + gated * gated
    return total


def gated_kernel(
    projc_ref, recv_ref, own_ref, fa_ref, fb_ref, a_ref, g_ref, gated_ref, total_ref, decays
):
    core = my_core()
    k = my_slice()
    decays[...] = joined_decay(recv_ref[COLS:, :])

    def keep(h, gated):
        gated_ref[h] = gated

    groups = (
        (own_ref, 4 * k, 4),
        (fa_ref, 4 * lax.bitwise_xor(k, 1 + 2 * core), 4),
        (fb_ref, 4 * lax.bitwise_xor(k, 2) + 2 * core, 2),
    )
    total_ref[...] = lifted_heads(
        groups, core == 1, decays, recv_ref, projc_ref[:, HD:], a_ref, g_ref,
        jnp.zeros((ROWS, HD), F32), keep,
    )


def last_gated_kernel(
    projc_ref, recv_ref, ha_ref, hb_ref, a_ref, g_ref, gated_in, total_ref,
    gated_ref, squares_ref, decays,
):
    del gated_in
    core = my_core()
    k = my_slice()
    decays[...] = joined_decay(recv_ref[COLS:, :])

    def keep(h, gated):
        gated_ref[h] = gated

    groups = (
        (ha_ref, 4 * lax.bitwise_xor(k, 3 - 2 * core), 4),
        (hb_ref, 4 * lax.bitwise_xor(k, 2) + 2 - 2 * core, 2),
    )
    total = lifted_heads(
        groups, core == 1, decays, recv_ref, projc_ref[:, HD:], a_ref, g_ref,
        total_ref[...], keep,
    )
    squares_ref[...] = jnp.broadcast_to(
        jnp.sum(total.T, axis=0, keepdims=True), (8, ROWS)
    )


def norm_kernel(gated_ref, s0, s1, s3, s2, gain_ref, out_hbm, out_ref, sems):
    total = (s0[0:1] + s1[0:1]) + (s2[0:1] + s3[0:1])
    scale = lax.rsqrt(total / (COLS * YS) + 1e-05)
    scale = jnp.broadcast_to(scale, (HD, ROWS)).T
    copies = []
    for i in range(HEADS):
        cols = slice(i * HD, (i + 1) * HD)
        out_ref[:, cols] = (gated_ref[i] * scale * gain_ref[0:1, cols]).astype(BF16)
        if i % 4 == 3:
            cols = pl.ds((i - 3) * HD, 4 * HD)
            copy = pltpu.make_async_copy(
                out_ref.at[:, cols], out_hbm.at[:, cols], sems.at[i // 4]
            )
            copy.start()
            copies.append(copy)
    for copy in copies:
        copy.wait()


VMEM = pl.BlockSpec(memory_space=pltpu.VMEM)
HBM = pl.BlockSpec(memory_space=pl.ANY)
DMA = pltpu.SemaphoreType.DMA


def shaped(*shape, dtype=BF16):
    return jax.ShapeDtypeStruct(shape, dtype)


def call(kernel, name, out, args, far=(), scratch=(), aliases=None, out_specs=None):
    single = not isinstance(out, (list, tuple))
    args = [
        pltpu.with_memory_space_constraint(x, pltpu.HBM) if i in far else x
        for i, x in enumerate(args)
    ]
    return pl.pallas_call(
        kernel,
        name=name,
        out_shape=out,
        in_specs=[HBM if i in far else VMEM for i in range(len(args))],
        out_specs=out_specs or (VMEM if single else [VMEM] * len(out)),
        scratch_shapes=list(scratch),
        input_output_aliases=aliases or {},
        compiler_params=pltpu.CompilerParams(vmem_limit_bytes=VMEM_LIMIT),
    )(*args)


def body(
    feat_in, gate_in, state_proj, step_raw, doc_offset, feat_taps, feat_bias,
    proj_taps, proj_bias, step_bias, decay_log, skip_gain, norm_gain,
):
    fbias = feat_bias.reshape(1, COLS)
    pbias = proj_bias.reshape(1, 256)
    gain = norm_gain.reshape(1, COLS)
    f32 = functools.partial(shaped, dtype=F32)

    params = [f32(TAPS, COLS), f32(1, COLS), f32(TAPS, 256), f32(1, 256)]
    edge, docv, feat, proj, *params, raw = call(
        edge_kernel, "edge",
        [
            shaped(16, PACK), shaped(8, HD, dtype=jnp.int32), shaped(ROWS, COLS),
            shaped(ROWS, 256), *params, f32(HEADS, ROWS),
        ],
        (doc_offset, feat_in, state_proj, feat_taps, fbias, proj_taps, pbias, step_raw),
        far=range(8),
        scratch=[pltpu.SMEM((ROWS,), jnp.int32), DMA((8,))],
    )
    rim = lax.ppermute(edge, "ctx", NEXT)

    featc, projc, cum, step, coef, decay = call(
        conv_kernel, "conv",
        [
            shaped(ROWS, COLS), shaped(ROWS, 256), f32(HEADS, ROWS), f32(HEADS, ROWS),
            f32(HEADS, ROWS), f32(HEADS, HD),
        ],
        (docv, feat, proj, *params, raw, step_bias, decay_log),
        far=(8, 9),
        scratch=[pltpu.SMEM((HEADS,), F32), pltpu.SMEM((HEADS,), F32), DMA((2,))],
    )
    featc, projc, keep, send = call(
        state_kernel, "state",
        [shaped(ROWS, COLS), shaped(ROWS, 256), f32(COLS, HD), shaped(COLS + 32, HD)],
        (docv, rim, feat, proj, *params, coef, decay, featc, projc),
        scratch=[pltpu.VMEM((32, COLS + 256), F32)],
        aliases={10: 0, 11: 1},
    )
    recv = lax.ppermute(send, "ctx", CORE)

    own, own_decay, ta, tb = call(
        chip_kernel, "chip",
        [f32(QUARTER, HD), f32(8, HD), shaped(QUARTER + 16, HD), shaped(2 * HD + 16, HD)],
        (keep, decay, recv),
        scratch=[pltpu.VMEM((40, HD), F32)],
    )
    rb = lax.ppermute(tb, "ctx", TWO)
    ra = lax.ppermute(ta, "ctx", APART)
    featc, projc, ta = lax.optimization_barrier((featc, projc, ta))
    a, g, gain = call(
        inner_kernel, "inner",
        [f32(HEADS, ROWS, HD), f32(HEADS, ROWS, HD), f32(1, COLS)],
        (docv, featc, projc, cum, step, gate_in, skip_gain, gain),
        far=(5, 6, 7),
        scratch=[
            pltpu.VMEM((ROWS, ROWS), F32),
            pltpu.VMEM((ROWS, COLS), BF16),
            pltpu.SMEM((HEADS,), F32),
            DMA((3,)),
        ],
    )
    ra, rb, a = lax.optimization_barrier((ra, rb, a))
    ga = lax.ppermute(ra, "ctx", CORE)
    gb = lax.ppermute(rb, "ctx", CORE)
    total, chips, decays = call(
        group_kernel, "group",
        [shaped(QUARTER + 16, HD), f32(4, QUARTER, HD), f32(4, 8, HD)],
        (own, own_decay, ra, ga, rb, gb),
    )
    q = lax.ppermute(total, "ctx", LATER)
    other = lax.ppermute(q, "ctx", CORE)
    e_own, ea, eb = call(
        enter_kernel, "enter",
        [f32(QUARTER, HD), shaped(QUARTER, HD), shaped(2 * HD, HD)],
        (chips, decays, q, other),
        scratch=[pltpu.VMEM((4, QUARTER, HD), F32)],
    )
    fb = lax.ppermute(eb, "ctx", TWO)
    fa = lax.ppermute(ea, "ctx", APART)
    ha = lax.ppermute(fa, "ctx", CORE)
    hb = lax.ppermute(fb, "ctx", CORE)
    gated, squares = call(
        gated_kernel, "gated", [f32(HEADS, ROWS, HD), f32(ROWS, HD)],
        (projc, recv, e_own, fa, fb, a, g), scratch=[pltpu.VMEM((HEADS, HD), F32)],
    )
    gated, squares = call(
        last_gated_kernel, "last_gated", [f32(HEADS, ROWS, HD), f32(8, ROWS)],
        (projc, recv, ha, hb, a, g, gated, squares),
        scratch=[pltpu.VMEM((HEADS, HD), F32)],
        aliases={6: 0},
    )
    s2 = lax.ppermute(squares, "head", HEAD_XOR[2])
    s3 = lax.ppermute(squares, "head", HEAD_XOR[3])
    s1 = lax.ppermute(squares, "head", HEAD_XOR[1])
    return call(
        norm_kernel, "norm", shaped(ROWS, COLS), (gated, squares, s1, s3, s2, gain),
        scratch=[pltpu.VMEM((ROWS, COLS), BF16), DMA((HEADS // 4,))],
        out_specs=HBM,
    )


def solution(mesh):
    return jax.shard_map(
        body,
        mesh=mesh,
        in_specs=(
            P("ctx", "head"),
            P("ctx", "head"),
            P("ctx", None),
            P("head", "ctx"),
            P("ctx"),
            P(None, "head"),
            P("head"),
            P(),
            P(),
            P("head"),
            P("head"),
            P("head"),
            P("head"),
        ),
        out_specs=P("ctx", "head"),
        check_vma=False,
    )
```

time: 205 us -> 56.5 us (0.28)
  waiting for transfers between devices: 137 us -> 25.4 us
  starting transfers between devices: 32.7 us -> 20.4 us
  other arithmetic: 11.9 us -> 0 us
  Pallas kernels: 0 us -> 10.4 us
  blocking collectives: 9.55 us -> 0 us
  local copies, waits for them, and re-layouts: 8.11 us -> 0 us
  matrix products: 4.84 us -> 0 us
    ppermute x11 -> x15, waiting for transfers between devices: 137 us -> 25.4 us  [the longest x1 6.02 us: body(): q = lax.ppermute(total, 'ctx', LATER)]
    ppermute x11 -> x15, starting transfers between devices: 32.7 us -> 20.4 us  [the longest x1 3.98 us: body(): q = lax.ppermute(total, 'ctx', LATER)]
    pallas_call x0 -> x10, Pallas kernels: none -> 10.4 us  [call(): pl.pallas_call(kernel, name=name, out_shape=out, in_specs=[HBM if i in fa...]
    all_to_all x1 -> x0, blocking collectives: 9.55 us -> none  [sent_to_all(): return lax.all_to_all(copies, axis, split_axis=0, concat_axis=0, tiled=True)]
    convert_element_type x6 -> x0, other arithmetic: 6.27 us -> none  [the longest x2 3.2 us: causal_taps(): return jax.nn.silu(summed).astype(jnp.bfloat16)]
    slice x8 -> x0, local copies, waits for them, and re-layouts: 5.53 us -> none  [the longest x2 1.79 us: causal_taps(): kernel_taps[tap_index][None, :] * window_rows]
    dot_general x4 -> x0, matrix products: 4.84 us -> none  [the longest x1 2.48 us: body(): jnp.einsum('tn,hpn->thp', out_block.astype(jnp.float32), start_state, pre...]
  transfers between devices with their start and end apart: 11 -> 15, of which waited for: 6 -> 12; matrix products, arithmetic and copies ran while one was open for 6% -> 0% of each run, Pallas kernels for 0% -> 11%
where the time goes in v1:
time: 56.5 us; the launch traced here: 56.3 us
  waiting for transfers between devices  25.4 us (45%)
  starting transfers between devices  20.4 us (36%)
  Pallas kernels  10.4 us (18%)
    pallas_call x10, Pallas kernels, call(): pl.pallas_call(kernel, name=name, out_shape=out, in_specs=[HBM if i in fa...  10.4 us
    ppermute x1, waiting for transfers between devices, body(): q = lax.ppermute(total, 'ctx', LATER)  6.02 us
    ppermute x1, waiting for transfers between devices, body(): rim = lax.ppermute(edge, 'ctx', NEXT)  4.31 us
    ppermute x1, starting transfers between devices, body(): q = lax.ppermute(total, 'ctx', LATER)  3.98 us
    ppermute x1, starting transfers between devices, body(): rb = lax.ppermute(tb, 'ctx', TWO)  3.73 us
    ppermute x1, starting transfers between devices, body(): s2 = lax.ppermute(squares, 'head', HEAD_XOR[2])  3.28 us
    ppermute x1, waiting for transfers between devices, body(): s3 = lax.ppermute(squares, 'head', HEAD_XOR[3])  2.9 us
    ppermute x1, waiting for transfers between devices, body(): fa = lax.ppermute(ea, 'ctx', APART)  2.66 us
  transfers between devices with their start and end apart: 15, of which 12 were waited for; matrix products, arithmetic and copies ran while one was open for 0% of the time, Pallas kernels for 11%

profile of v1, /device:TPU:6, one launch (start us, length us, event | category | flops | bytes accessed | tf_op | source)
XLA Modules:
  0.0 56.3 jit_solution(4951768210976716319)
XLA Ops:
  0.0 1.3 %edge.1 = (bf16[16,640]{1,0:T(8,128)(2,1)S(1)}, s32[8,128]{1,0:T(8,128)S(1)}, bf16[256,2048]{1,0:T(8,128)(2,1)S(1)}, bf16[256,256]{1,0:T(8,128)(2,1)S(1)}, f32[4...) custom-call(s32[256]{0:T(256)} %doc_hbm.1, ...), custom_call_target="tpu_custom_call" | custom-call | tf_op jit(solution)/shard_map/edge/pallas_call | solution.py:467
  1.3 1.9 %collective-permute-start = (bf16[16,640]{1,0:T(8,128)(2,1)S(1)}, bf16[16,640]{1,0:T(8,128)(2,1)S(1)}, u32[]{:S(2)}, u32[]{:S(2)}) collective-permute-start(bf16[16,640]{1,0:T(8,128)(2,1)S(1)} %get-tuple-element.47), channel_id=1, source_target_pairs={{0,4},{4,8},{8,12},{12,16},{16,20},{20,24},{24,28},{28,32},{32,36}... | collective-permute-start | bytes 61448 | tf_op jit(solution)/shard_map/ppermute | solution.py:499
  3.3 2.7 %conv.1 = (bf16[256,2048]{1,0:T(8,128)(2,1)S(1)}, bf16[256,256]{1,0:T(8,128)(2,1)S(1)}, f32[16,256]{1,0:T(8,128)S(1)}, f32[16,256]{1,0:T(8,128)S(1)}, f32[16,256]{1,0:T(8,128)S(1)}, /*index=5*/f32[16,128]{1,0:T(8,128)S(1)}) custom-call(s32[8,128]{1,0:T(8,128)S(1)} %get-tuple-element.46.docv_ref, bf16[256,2048]{1,0:T(8,128)(2,1)S(1)} %get-tuple-element.48.feat_ref, ...), custom_call_target="tpu_custom_call" | custom-call | tf_op jit(solution)/shard_map/conv/pallas_call | solution.py:467
  6.0 4.3 %collective-permute-done.rim_ref = bf16[16,640]{1,0:T(8,128)(2,1)S(1)} collective-permute-done((bf16[16,640]{1,0:T(8,128)(2,1)S(1)}, bf16[16,640]{1,0:T(8,128)(2,1)S(1)}, u32[]{:S(2)}, u32[]{:S(2)}) %collective-permute-start) | collective-permute-done | bytes 20512 | tf_op jit(solution)/shard_map/ppermute | solution.py:499
  10.3 0.7 %state.1 = (bf16[256,2048]{1,0:T(8,128)(2,1)S(1)}, bf16[256,256]{1,0:T(8,128)(2,1)S(1)}, f32[2048,128]{1,0:T(8,128)S(1)}, bf16[2080,128]{1,0:T(8,128)(2,1)S(1)}) custom-call(s32[8,128]{1,0:T(8,128)S(1)} %get-tuple-element.46.docv_ref, bf16[16,640]{1,0:T(8,128)(2,1)S(1)} %collective-permute-done.rim_ref, ...), custom_call_target="tpu_custom_call", output_to_operand_aliasing={{0}: (10, {}), {1}: (11, {})} | custom-call | tf_op jit(solution)/shard_map/state/pallas_call | solution.py:467
  11.0 1.9 %collective-permute-done.1.recv_ref = bf16[2080,128]{1,0:T(8,128)(2,1)S(1)} collective-permute-done((bf16[2080,128]{1,0:T(8,128)(2,1)S(1)}, bf16[2080,128]{1,0:T(8,128)(2,1)S(1)}, u32[]{:S(2)}, u32[]{:S(2)}) %collective-permute-start.1) | collective-permute-done | bytes 532512 | tf_op jit(solution)/shard_map/ppermute | solution.py:518
  13.2 3.7 %collective-permute-start.3 = (bf16[272,128]{1,0:T(8,128)(2,1)S(1)}, bf16[272,128]{1,0:T(8,128)(2,1)S(1)}, u32[]{:S(2)}, u32[]{:S(2)}) collective-permute-start(bf16[272,128]{1,0:T(8,128)(2,1)S(1)} %get-tuple-element.67), channel_id=1, source_target_pairs={{0,16},{4,20},{8,24},{12,28},{16,0},{20,4},{24,8},{28,12},{32,48},... | collective-permute-start | bytes 208904 | tf_op jit(solution)/shard_map/ppermute | solution.py:526
  16.9 2.9 %inner.1 = (f32[16,256,128]{2,1,0:T(8,128)S(1)}, f32[16,256,128]{2,1,0:T(8,128)S(1)}, f32[1,2048]{1,0:T(1,128)S(1)}) custom-call(s32[8,128]{1,0:T(8,128)S(1)} %get-tuple-element.46.docv_ref, bf16[256,2048]{1,0:T(8,128)(2,1)S(1)} %get-tuple-element.68.featc_ref, bf16[256,256]{1,0:T(8,128)(2,1)S(1)} %get-tuple-element.64.projc_ref, ...), custom_call_target="tpu_custom_call" | custom-call | tf_op jit(solution)/shard_map/inner/pallas_call | solution.py:467
  20.0 0.8 %collective-permute-done.2.ra_ref = bf16[528,128]{1,0:T(8,128)(2,1)S(1)} collective-permute-done((bf16[528,128]{1,0:T(8,128)(2,1)S(1)}, bf16[528,128]{1,0:T(8,128)(2,1)S(1)}, u32[]{:S(2)}, u32[]{:S(2)}) %collective-permute-start.2) | collective-permute-done | bytes 135200 | tf_op jit(solution)/shard_map/ppermute | solution.py:527
  20.8 1.4 %collective-permute-start.4 = (bf16[528,128]{1,0:T(8,128)(2,1)S(1)}, bf16[528,128]{1,0:T(8,128)(2,1)S(1)}, u32[]{:S(2)}, u32[]{:S(2)}) collective-permute-start(bf16[528,128]{1,0:T(8,128)(2,1)S(1)} %collective-permute-done.2.ra_ref), channel_id=1, source_target_pairs={{0,4},{4,0},{8,12},{12,8},{16,20},{20,16},{24,28},{28,24},{32,36},... | collective-permute-start | bytes 405512 | tf_op jit(solution)/shard_map/ppermute | solution.py:542
  22.2 1.3 %collective-permute-done.5.gb_ref = bf16[272,128]{1,0:T(8,128)(2,1)S(1)} collective-permute-done((bf16[272,128]{1,0:T(8,128)(2,1)S(1)}, bf16[272,128]{1,0:T(8,128)(2,1)S(1)}, u32[]{:S(2)}, u32[]{:S(2)}) %collective-permute-start.5) | collective-permute-done | bytes 69664 | tf_op jit(solution)/shard_map/ppermute | solution.py:543
  23.7 4.0 %collective-permute-start.6 = (bf16[528,128]{1,0:T(8,128)(2,1)S(1)}, bf16[528,128]{1,0:T(8,128)(2,1)S(1)}, u32[]{:S(2)}, u32[]{:S(2)}) collective-permute-start(bf16[528,128]{1,0:T(8,128)(2,1)S(1)} %get-tuple-element.76), channel_id=1, source_target_pairs={{0,48},{4,68},{8,56},{12,76},{16,32},{20,84},{24,40},{28,92},{32,8... | collective-permute-start | bytes 405512 | tf_op jit(solution)/shard_map/ppermute | solution.py:549
  27.7 6.0 %collective-permute-done.6.q_ref = bf16[528,128]{1,0:T(8,128)(2,1)S(1)} collective-permute-done((bf16[528,128]{1,0:T(8,128)(2,1)S(1)}, bf16[528,128]{1,0:T(8,128)(2,1)S(1)}, u32[]{:S(2)}, u32[]{:S(2)}) %collective-permute-start.6) | collective-permute-done | bytes 135200 | tf_op jit(solution)/shard_map/ppermute | solution.py:549
  33.7 1.4 %collective-permute-done.7.other_ref = bf16[528,128]{1,0:T(8,128)(2,1)S(1)} collective-permute-done((bf16[528,128]{1,0:T(8,128)(2,1)S(1)}, bf16[528,128]{1,0:T(8,128)(2,1)S(1)}, u32[]{:S(2)}, u32[]{:S(2)}) %collective-permute-start.7) | collective-permute-done | bytes 135200 | tf_op jit(solution)/shard_map/ppermute | solution.py:550
  35.2 2.1 %collective-permute-start.8 = (bf16[512,128]{1,0:T(8,128)(2,1)S(1)}, bf16[512,128]{1,0:T(8,128)(2,1)S(1)}, u32[]{:S(2)}, u32[]{:S(2)}) collective-permute-start(bf16[512,128]{1,0:T(8,128)(2,1)S(1)} %get-tuple-element.77), channel_id=1, source_target_pairs={{0,8},{4,28},{8,0},{12,20},{16,24},{20,12},{24,16},{28,4},{32,40},... | collective-permute-start | bytes 393224 | tf_op jit(solution)/shard_map/ppermute | solution.py:558
  37.4 1.2 %collective-permute-start.10 = (bf16[256,128]{1,0:T(8,128)(2,1)S(1)}, bf16[256,128]{1,0:T(8,128)(2,1)S(1)}, u32[]{:S(2)}, u32[]{:S(2)}) collective-permute-start(bf16[256,128]{1,0:T(8,128)(2,1)S(1)} %get-tuple-element.78), channel_id=1, source_target_pairs={{0,16},{4,20},{8,24},{12,28},{16,0},{20,4},{24,8},{28,12},{32,48},... | collective-permute-start | bytes 196616 | tf_op jit(solution)/shard_map/ppermute | solution.py:557
  38.6 2.7 %collective-permute-done.8.fa_ref = bf16[512,128]{1,0:T(8,128)(2,1)S(1)} collective-permute-done((bf16[512,128]{1,0:T(8,128)(2,1)S(1)}, bf16[512,128]{1,0:T(8,128)(2,1)S(1)}, u32[]{:S(2)}, u32[]{:S(2)}) %collective-permute-start.8) | collective-permute-done | bytes 131104 | tf_op jit(solution)/shard_map/ppermute | solution.py:558
  41.3 1.3 %collective-permute-start.9 = (bf16[512,128]{1,0:T(8,128)(2,1)S(1)}, bf16[512,128]{1,0:T(8,128)(2,1)S(1)}, u32[]{:S(2)}, u32[]{:S(2)}) collective-permute-start(bf16[512,128]{1,0:T(8,128)(2,1)S(1)} %collective-permute-done.8.fa_ref), channel_id=1, source_target_pairs={{0,4},{4,0},{8,12},{12,8},{16,20},{20,16},{24,28},{28,24},{32,36},... | collective-permute-start | bytes 393224 | tf_op jit(solution)/shard_map/ppermute | solution.py:559
  42.6 2.5 %collective-permute-done.10.fb_ref = bf16[256,128]{1,0:T(8,128)(2,1)S(1)} collective-permute-done((bf16[256,128]{1,0:T(8,128)(2,1)S(1)}, bf16[256,128]{1,0:T(8,128)(2,1)S(1)}, u32[]{:S(2)}, u32[]{:S(2)}) %collective-permute-start.10) | collective-permute-done | bytes 65568 | tf_op jit(solution)/shard_map/ppermute | solution.py:557
  46.9 3.3 %collective-permute-start.14 = (f32[8,256]{1,0:T(8,128)S(1)}, f32[8,256]{1,0:T(8,128)S(1)}, u32[]{:S(2)}, u32[]{:S(2)}) collective-permute-start(f32[8,256]{1,0:T(8,128)S(1)} %get-tuple-element.85.s0), channel_id=1, source_target_pairs={{0,2},{1,3},{2,0},{3,1},{4,6},{5,7},{6,4},{7,5},{8,10},{9,11},{10,... | collective-permute-start | bytes 24584 | tf_op jit(solution)/shard_map/ppermute | solution.py:571
  50.2 1.1 %collective-permute-start.13 = (f32[8,256]{1,0:T(8,128)S(1)}, f32[8,256]{1,0:T(8,128)S(1)}, u32[]{:S(2)}, u32[]{:S(2)}) collective-permute-start(f32[8,256]{1,0:T(8,128)S(1)} %get-tuple-element.85.s0), channel_id=1, source_target_pairs={{0,3},{1,2},{2,1},{3,0},{4,7},{5,6},{6,5},{7,4},{8,11},{9,10},{10,... | collective-permute-start | bytes 24584 | tf_op jit(solution)/shard_map/ppermute | solution.py:572
  51.2 0.9 %collective-permute-done.14.s2 = f32[8,256]{1,0:T(8,128)S(1)} collective-permute-done((f32[8,256]{1,0:T(8,128)S(1)}, f32[8,256]{1,0:T(8,128)S(1)}, u32[]{:S(2)}, u32[]{:S(2)}) %collective-permute-start.14) | collective-permute-done | bytes 8224 | tf_op jit(solution)/shard_map/ppermute | solution.py:571
  52.1 2.9 %collective-permute-done.13.s3 = f32[8,256]{1,0:T(8,128)S(1)} collective-permute-done((f32[8,256]{1,0:T(8,128)S(1)}, f32[8,256]{1,0:T(8,128)S(1)}, u32[]{:S(2)}, u32[]{:S(2)}) %collective-permute-start.13) | collective-permute-done | bytes 8224 | tf_op jit(solution)/shard_map/ppermute | solution.py:572
  55.0 1.3 %norm.1 = bf16[256,2048]{1,0:T(8,128)(2,1)} custom-call(f32[16,256,128]{2,1,0:T(8,128)S(1)} %get-tuple-element.84.gated_ref, f32[8,256]{1,0:T(8,128)S(1)} %get-tuple-element.85.s0, f32[8,256]{1,0:T(8,128)S(1)} %collective-permute-done.12.s1, f32[8,256]{1,0:T(8,128)S(1)} %collective-permute-done.13.s3, f32[8,256]{1,0:T(8,128)S(1)} %collective-permute-done.14.s2, ...), custom_call_target="tpu_custom_call" | custom-call | tf_op jit(solution)/shard_map/norm/pallas_call | solution.py:467
  (16 shorter events, 2.6 us)
Async XLA Ops:
  1.3 8.9 %collective-permute-start = (bf16[16,640]{1,0:T(8,128)(2,1)S(1)}, bf16[16,640]{1,0:T(8,128)(2,1)S(1)}, u32[]{:S(2)}, u32[]{:S(2)}) collective-permute-start(bf16[16,640]{1,0:T(8,128)(2,1)S(1)} %get-tuple-element.47), channel_id=1, source_target_pairs={{0,4},{4,8},{8,12},{12,16},{16,20},{20,24},{24,28},{28,32},{32,36}... | collective-permute-start | bytes 61448 | tf_op jit(solution)/shard_map/ppermute | solution.py:499
  10.9 2.0 %collective-permute-start.1 = (bf16[2080,128]{1,0:T(8,128)(2,1)S(1)}, bf16[2080,128]{1,0:T(8,128)(2,1)S(1)}, u32[]{:S(2)}, u32[]{:S(2)}) collective-permute-start(bf16[2080,128]{1,0:T(8,128)(2,1)S(1)} %get-tuple-element.62), channel_id=1, source_target_pairs={{0,4},{4,0},{8,12},{12,8},{16,20},{20,16},{24,28},{28,24},{32,36},... | collective-permute-start | bytes 1597448 | tf_op jit(solution)/shard_map/ppermute | solution.py:518
  13.1 7.7 %collective-permute-start.2 = (bf16[528,128]{1,0:T(8,128)(2,1)S(1)}, bf16[528,128]{1,0:T(8,128)(2,1)S(1)}, u32[]{:S(2)}, u32[]{:S(2)}) collective-permute-start(bf16[528,128]{1,0:T(8,128)(2,1)S(1)} %get-tuple-element.63), channel_id=1, source_target_pairs={{0,8},{4,28},{8,0},{12,20},{16,24},{20,12},{24,16},{28,4},{32,40},... | collective-permute-start | bytes 405512 | tf_op jit(solution)/shard_map/ppermute | solution.py:527
  13.2 6.8 %collective-permute-start.3 = (bf16[272,128]{1,0:T(8,128)(2,1)S(1)}, bf16[272,128]{1,0:T(8,128)(2,1)S(1)}, u32[]{:S(2)}, u32[]{:S(2)}) collective-permute-start(bf16[272,128]{1,0:T(8,128)(2,1)S(1)} %get-tuple-element.67), channel_id=1, source_target_pairs={{0,16},{4,20},{8,24},{12,28},{16,0},{20,4},{24,8},{28,12},{32,48},... | collective-permute-start | bytes 208904 | tf_op jit(solution)/shard_map/ppermute | solution.py:526
  20.8 2.7 %collective-permute-start.4 = (bf16[528,128]{1,0:T(8,128)(2,1)S(1)}, bf16[528,128]{1,0:T(8,128)(2,1)S(1)}, u32[]{:S(2)}, u32[]{:S(2)}) collective-permute-start(bf16[528,128]{1,0:T(8,128)(2,1)S(1)} %collective-permute-done.2.ra_ref), channel_id=1, source_target_pairs={{0,4},{4,0},{8,12},{12,8},{16,20},{20,16},{24,28},{28,24},{32,36},... | collective-permute-start | bytes 405512 | tf_op jit(solution)/shard_map/ppermute | solution.py:542
  22.2 1.3 %collective-permute-start.5 = (bf16[272,128]{1,0:T(8,128)(2,1)S(1)}, bf16[272,128]{1,0:T(8,128)(2,1)S(1)}, u32[]{:S(2)}, u32[]{:S(2)}) collective-permute-start(bf16[272,128]{1,0:T(8,128)(2,1)S(1)} %collective-permute-done.3.rb_ref), channel_id=1, source_target_pairs={{0,4},{4,0},{8,12},{12,8},{16,20},{20,16},{24,28},{28,24},{32,36},... | collective-permute-start | bytes 208904 | tf_op jit(solution)/shard_map/ppermute | solution.py:543
  23.7 10.0 %collective-permute-start.6 = (bf16[528,128]{1,0:T(8,128)(2,1)S(1)}, bf16[528,128]{1,0:T(8,128)(2,1)S(1)}, u32[]{:S(2)}, u32[]{:S(2)}) collective-permute-start(bf16[528,128]{1,0:T(8,128)(2,1)S(1)} %get-tuple-element.76), channel_id=1, source_target_pairs={{0,48},{4,68},{8,56},{12,76},{16,32},{20,84},{24,40},{28,92},{32,8... | collective-permute-start | bytes 405512 | tf_op jit(solution)/shard_map/ppermute | solution.py:549
  33.7 1.4 %collective-permute-start.7 = (bf16[528,128]{1,0:T(8,128)(2,1)S(1)}, bf16[528,128]{1,0:T(8,128)(2,1)S(1)}, u32[]{:S(2)}, u32[]{:S(2)}) collective-permute-start(bf16[528,128]{1,0:T(8,128)(2,1)S(1)} %collective-permute-done.6.q_ref), channel_id=1, source_target_pairs={{0,4},{4,0},{8,12},{12,8},{16,20},{20,16},{24,28},{28,24},{32,36},... | collective-permute-start | bytes 405512 | tf_op jit(solution)/shard_map/ppermute | solution.py:550
  35.2 6.0 %collective-permute-start.8 = (bf16[512,128]{1,0:T(8,128)(2,1)S(1)}, bf16[512,128]{1,0:T(8,128)(2,1)S(1)}, u32[]{:S(2)}, u32[]{:S(2)}) collective-permute-start(bf16[512,128]{1,0:T(8,128)(2,1)S(1)} %get-tuple-element.77), channel_id=1, source_target_pairs={{0,8},{4,28},{8,0},{12,20},{16,24},{20,12},{24,16},{28,4},{32,40},... | collective-permute-start | bytes 393224 | tf_op jit(solution)/shard_map/ppermute | solution.py:558
  37.4 7.7 %collective-permute-start.10 = (bf16[256,128]{1,0:T(8,128)(2,1)S(1)}, bf16[256,128]{1,0:T(8,128)(2,1)S(1)}, u32[]{:S(2)}, u32[]{:S(2)}) collective-permute-start(bf16[256,128]{1,0:T(8,128)(2,1)S(1)} %get-tuple-element.78), channel_id=1, source_target_pairs={{0,16},{4,20},{8,24},{12,28},{16,0},{20,4},{24,8},{28,12},{32,48},... | collective-permute-start | bytes 196616 | tf_op jit(solution)/shard_map/ppermute | solution.py:557
  41.3 5.1 %collective-permute-start.9 = (bf16[512,128]{1,0:T(8,128)(2,1)S(1)}, bf16[512,128]{1,0:T(8,128)(2,1)S(1)}, u32[]{:S(2)}, u32[]{:S(2)}) collective-permute-start(bf16[512,128]{1,0:T(8,128)(2,1)S(1)} %collective-permute-done.8.fa_ref), channel_id=1, source_target_pairs={{0,4},{4,0},{8,12},{12,8},{16,20},{20,16},{24,28},{28,24},{32,36},... | collective-permute-start | bytes 393224 | tf_op jit(solution)/shard_map/ppermute | solution.py:559
  45.1 1.3 %collective-permute-start.11 = (bf16[256,128]{1,0:T(8,128)(2,1)S(1)}, bf16[256,128]{1,0:T(8,128)(2,1)S(1)}, u32[]{:S(2)}, u32[]{:S(2)}) collective-permute-start(bf16[256,128]{1,0:T(8,128)(2,1)S(1)} %collective-permute-done.10.fb_ref), channel_id=1, source_target_pairs={{0,4},{4,0},{8,12},{12,8},{16,20},{20,16},{24,28},{28,24},{32,36},... | collective-permute-start | bytes 196616 | tf_op jit(solution)/shard_map/ppermute | solution.py:560
  46.9 5.2 %collective-permute-start.14 = (f32[8,256]{1,0:T(8,128)S(1)}, f32[8,256]{1,0:T(8,128)S(1)}, u32[]{:S(2)}, u32[]{:S(2)}) collective-permute-start(f32[8,256]{1,0:T(8,128)S(1)} %get-tuple-element.85.s0), channel_id=1, source_target_pairs={{0,2},{1,3},{2,0},{3,1},{4,6},{5,7},{6,4},{7,5},{8,10},{9,11},{10,... | collective-permute-start | bytes 24584 | tf_op jit(solution)/shard_map/ppermute | solution.py:571
  50.2 4.9 %collective-permute-start.13 = (f32[8,256]{1,0:T(8,128)S(1)}, f32[8,256]{1,0:T(8,128)S(1)}, u32[]{:S(2)}, u32[]{:S(2)}) collective-permute-start(f32[8,256]{1,0:T(8,128)S(1)} %get-tuple-element.85.s0), channel_id=1, source_target_pairs={{0,3},{1,2},{2,1},{3,0},{4,7},{5,6},{6,5},{7,4},{8,11},{9,10},{10,... | collective-permute-start | bytes 24584 | tf_op jit(solution)/shard_map/ppermute | solution.py:572
  51.2 3.8 %collective-permute-start.12 = (f32[8,256]{1,0:T(8,128)S(1)}, f32[8,256]{1,0:T(8,128)S(1)}, u32[]{:S(2)}, u32[]{:S(2)}) collective-permute-start(f32[8,256]{1,0:T(8,128)S(1)} %get-tuple-element.85.s0), channel_id=1, source_target_pairs={{0,1},{1,0},{2,3},{3,2},{4,5},{5,4},{6,7},{7,6},{8,9},{9,8},{10,11... | collective-permute-start | bytes 24584 | tf_op jit(solution)/shard_map/ppermute | solution.py:573

commit v2 on v1

--- a/solution.py
+++ b/solution.py
@@ -76,6 +76,23 @@
     return half + half * jnp.tanh(half)
 
 
+SOON = 10
+
+
+def order_of(core):
+    k = my_slice()
+    apart = lax.bitwise_xor(k, 1 + 2 * core)
+    two = 4 * lax.bitwise_xor(k, 2)
+    later = lax.bitwise_xor(k, 3 - 2 * core)
+    return (
+        [4 * k + i for i in range(4)]
+        + [4 * apart + i for i in range(4)]
+        + [two + 2 * core + i for i in range(2)]
+        + [4 * later + i for i in range(4)]
+        + [two + 2 - 2 * core + i for i in range(2)]
+    )
+
+
 def conv_rows(xs, taps_ref, bias_ref, cols, scratch_cols, base, rows, masks):
     acc = jnp.broadcast_to(bias_ref[0:1, cols], (rows, HD))
     for k in range(TAPS):
@@ -93,15 +110,20 @@
 
 def edge_kernel(
     doc_hbm, feat_hbm, proj_hbm, ftaps_hbm, fbias_hbm, ptaps_hbm, pbias_hbm, raw_hbm,
+    sbias_hbm, dlog_hbm,
     out_ref, docv_ref, feat_ref, proj_ref, ftaps_ref, fbias_ref, ptaps_ref, pbias_ref, raw_ref,
-    doc_ref, sems,
-):
+    bias_ref, speed_ref, doc_ref, sbias_ref, dlog_ref, sems,
+):
+    tail = pl.ds(ROWS - 16, 16)
+    bulk = pl.ds(0, ROWS - 16)
     copies = [
         pltpu.make_async_copy(source, target, sems.at[n])
         for n, (source, target) in enumerate((
-            (feat_hbm, feat_ref), (proj_hbm, proj_ref), (doc_hbm, doc_ref),
+            (feat_hbm.at[tail, :], feat_ref.at[tail, :]), (proj_hbm, proj_ref),
+            (feat_hbm.at[bulk, :], feat_ref.at[bulk, :]), (doc_hbm, doc_ref),
             (ftaps_hbm, ftaps_ref), (fbias_hbm, fbias_ref), (ptaps_hbm, ptaps_ref),
-            (pbias_hbm, pbias_ref), (raw_hbm, raw_ref),
+            (pbias_hbm, pbias_ref), (raw_hbm, raw_ref), (sbias_hbm, sbias_ref),
+            (dlog_hbm, dlog_ref),
         ))
     ]
     for copy in copies:
@@ -124,6 +146,14 @@
         copy.wait()
     row = lax.broadcasted_iota(jnp.int32, (8, HD), 0)
     docv_ref[...] = jnp.where(row == 0, doc_ref[0], (ROWS - 1) - doc_ref[ROWS - 1])
+    line = lax.broadcasted_iota(jnp.int32, (HEADS, HD), 0)
+    bias = jnp.zeros((HEADS, HD), F32)
+    speed = jnp.zeros((HEADS, HD), F32)
+    for h in range(HEADS):
+        bias = jnp.where(line == h, sbias_ref[h], bias)
+        speed = jnp.where(line == h, dlog_ref[h], speed)
+    bias_ref[...] = bias
+    speed_ref[...] = speed
 
 
 def split_decay(value):
@@ -139,15 +169,9 @@
 
 def conv_kernel(
     docv_ref, feat_ref, proj_ref, ftaps_ref, fbias_ref, ptaps_ref, pbias_ref, raw_ref,
-    sbias_hbm, dlog_hbm,
-    featc_ref, projc_ref, cum_ref, step_ref, coef_ref, decay_ref, sbias_ref, dlog_ref, sems,
-):
-    copies = [
-        pltpu.make_async_copy(sbias_hbm, sbias_ref, sems.at[0]),
-        pltpu.make_async_copy(dlog_hbm, dlog_ref, sems.at[1]),
-    ]
-    for copy in copies:
-        copy.start()
+    sbias_ref, speed_ref,
+    featc_ref, projc_ref, cum_ref, step_ref, coef_ref, decay_ref,
+):
     first, start = docv_ref[0:1], docv_ref[1:2]
     first = jnp.concatenate([first, first], axis=1)
     start = jnp.concatenate([start, start], axis=1)
@@ -172,26 +196,19 @@
                 acc = acc + taps_ref[k : k + 1, cols] * moved
             out_ref[:, cols] = silu(acc).astype(BF16)
 
-    conv(proj_ref, ptaps_ref, pbias_ref, projc_ref)
-    conv(feat_ref, ftaps_ref, fbias_ref, featc_ref)
-
-    for copy in copies:
-        copy.wait()
     first, start = first[:, 0:1], start[:, 0:1]
-    line = lax.broadcasted_iota(jnp.int32, (HEADS, ROWS), 0)
     lane = lax.broadcasted_iota(jnp.int32, (HEADS, ROWS), 1)
-    bias = jnp.zeros((HEADS, ROWS), F32)
-    speed = jnp.zeros((HEADS, ROWS), F32)
-    for h in range(HEADS):
-        bias = jnp.where(line == h, sbias_ref[h], bias)
-        speed = jnp.where(line == h, dlog_ref[h], speed)
-    v = raw_ref[...] + bias
+    bias = sbias_ref[...]
+    speed = jnp.exp(speed_ref[...])
+    v = raw_ref[...] + jnp.concatenate([bias, bias], axis=1)
     step = jnp.maximum(v, 0.0) + jnp.log1p(jnp.exp(-jnp.abs(v)))
-    cum = -step * jnp.exp(speed)
+    cum = -step * jnp.concatenate([speed, speed], axis=1)
     shift = 1
     while shift < ROWS:
         cum = cum + jnp.where(lane >= shift, pltpu.roll(cum, shift, 1), 0.0)
         shift *= 2
+    conv(proj_ref, ptaps_ref, pbias_ref, projc_ref)
+    conv(feat_ref, ftaps_ref, fbias_ref, featc_ref)
     last = cum[:, ROWS - 1 : ROWS]
     cum_ref[...] = cum
     step_ref[...] = step
@@ -204,7 +221,7 @@
 def state_kernel(
     docv_ref, rim_ref, feat_ref, proj_ref, ftaps_ref, fbias_ref, ptaps_ref, pbias_ref,
     coef_ref, decay_ref, featc_in, projc_in,
-    featc_ref, projc_ref, keep_ref, send_ref, xs,
+    featc_ref, projc_ref, keep_ref, send_ref, rest_ref, xs,
 ):
     del featc_in, projc_in
     rim = rim_ref[...].astype(F32)
@@ -226,41 +243,44 @@
         cols = slice(j * HD, (j + 1) * HD)
         featc_ref[0:16, cols] = conv_rows(xs, ftaps_ref, fbias_ref, cols, cols, 16, 16, masks)
     turned = projc_ref[:, :HD].astype(F32).T
-    for h in range(HEADS):
-        rows = slice(h * HD, (h + 1) * HD)
-        scaled = (turned * coef_ref[h : h + 1, :]).astype(BF16)
+    for n, h in enumerate(order_of(1 - my_core())):
+        rows = pl.ds(pl.multiple_of(h * HD, HD), HD)
+        scaled = (turned * coef_ref[pl.ds(h, 1), :]).astype(BF16)
         added = jnp.dot(scaled, featc_ref[:, rows], preferred_element_type=F32)
         keep_ref[rows, :] = added
-        send_ref[rows, :] = added.astype(BF16)
-    send_ref[COLS:, :] = split_decay(decay_ref[...])
+        if n < SOON:
+            send_ref[n * HD : (n + 1) * HD, :] = added.astype(BF16)
+        else:
+            rest_ref[(n - SOON) * HD : (n - SOON + 1) * HD, :] = added.astype(BF16)
+    send_ref[SOON * HD :, :] = split_decay(decay_ref[...])
 
 
 def chip_kernel(keep_ref, decay_ref, recv_ref, own_ref, own_decay_ref, a_ref, b_ref, decays):
     core = my_core()
     second = core == 1
     k = my_slice()
-    theirs = joined_decay(recv_ref[COLS:, :])
+    theirs = joined_decay(recv_ref[SOON * HD :, :])
     mine = decay_ref[...]
     decays[0:16, :] = jnp.where(second, mine, theirs)
     decays[16:32, :] = mine * theirs
     decays[32:40, :] = jnp.zeros((8, HD), F32)
 
-    def combined(h):
-        rows = pl.ds(pl.multiple_of(h * HD, HD), HD)
-        a = keep_ref[rows, :]
-        b = recv_ref[rows, :].astype(F32)
+    order = order_of(core)
+
+    def combined(n):
+        h = order[n]
+        a = keep_ref[pl.ds(pl.multiple_of(h * HD, HD), HD), :]
+        b = recv_ref[n * HD : (n + 1) * HD, :].astype(F32)
         return decays[pl.ds(h, 1), :] * jnp.where(second, b, a) + jnp.where(second, a, b)
 
-    s = lax.bitwise_xor(k, 1 + 2 * core)
     for i in range(4):
-        a_ref[i * HD : (i + 1) * HD, :] = combined(4 * s + i).astype(BF16)
-    a_ref[4 * HD :, :] = split_decay(decays[pl.ds(16 + 4 * s, 8), :])
-    s = lax.bitwise_xor(k, 2)
+        a_ref[i * HD : (i + 1) * HD, :] = combined(4 + i).astype(BF16)
+    a_ref[4 * HD :, :] = split_decay(decays[pl.ds(16 + order[4], 8), :])
     for i in range(2):
-        b_ref[i * HD : (i + 1) * HD, :] = combined(4 * s + 2 * core + i).astype(BF16)
-    b_ref[2 * HD :, :] = split_decay(decays[pl.ds(16 + 4 * s, 8), :])
+        b_ref[i * HD : (i + 1) * HD, :] = combined(8 + i).astype(BF16)
+    b_ref[2 * HD :, :] = split_decay(decays[pl.ds(16 + 4 * lax.bitwise_xor(k, 2), 8), :])
     for i in range(4):
-        own_ref[i * HD : (i + 1) * HD, :] = combined(4 * k + i)
+        own_ref[i * HD : (i + 1) * HD, :] = combined(i)
     own_decay_ref[...] = decays[pl.ds(16 + 4 * k, 8), :]
 
 
@@ -365,65 +385,45 @@
             a_ref[h, top : top + HD, :] = (inner + skip_ref[h] * feat) * gate[top : top + HD]
 
 
-def lifted_heads(groups, second, decays, recv_ref, c, a_ref, g_ref, total, keep):
-    for ref, base, count in groups:
-        for i in range(count):
-            h = base + i
-            rows = pl.ds(pl.multiple_of(h * HD, HD), HD)
-            state = ref[i * HD : (i + 1) * HD, :].astype(F32)
-            middle = decays[pl.ds(h, 1), :] * state + recv_ref[rows, :].astype(F32)
-            state = jnp.where(second, middle, state)
-            high = state.astype(BF16)
-            low = (state - high.astype(F32)).astype(BF16)
-            lifted = jnp.dot(c, high, preferred_element_type=F32) + jnp.dot(
-                c, low, preferred_element_type=F32
-            )
-            gated = a_ref[h] + lifted * g_ref[h]
-            keep(h, gated)
-            total = total + gated * gated
+def lifted_heads(refs, heads, early_ref, decays, c, a_ref, g_ref, gated_ref, total):
+    second = my_core() == 1
+    states = [
+        ref[i * HD : (i + 1) * HD, :] for ref in refs for i in range(ref.shape[0] // HD)
+    ]
+    for n, (h, state) in enumerate(zip(heads, states, strict=True)):
+        state = state.astype(F32)
+        early = early_ref[n * HD : (n + 1) * HD, :].astype(F32)
+        state = jnp.where(second, decays[pl.ds(h, 1), :] * state + early, state)
+        high = state.astype(BF16)
+        low = (state - high.astype(F32)).astype(BF16)
+        lifted = jnp.dot(c, high, preferred_element_type=F32) + jnp.dot(
+            c, low, preferred_element_type=F32
+        )
+        gated = a_ref[h] + lifted * g_ref[h]
+        gated_ref[h] = gated
+        total = total + gated * gated
     return total
 
 
 def gated_kernel(
-    projc_ref, recv_ref, own_ref, fa_ref, fb_ref, a_ref, g_ref, gated_ref, total_ref, decays
-):
-    core = my_core()
-    k = my_slice()
-    decays[...] = joined_decay(recv_ref[COLS:, :])
-
-    def keep(h, gated):
-        gated_ref[h] = gated
-
-    groups = (
-        (own_ref, 4 * k, 4),
-        (fa_ref, 4 * lax.bitwise_xor(k, 1 + 2 * core), 4),
-        (fb_ref, 4 * lax.bitwise_xor(k, 2) + 2 * core, 2),
-    )
+    projc_ref, recv_ref, own_ref, fa_ref, fb_ref, a_ref, g_ref,
+    gated_ref, total_ref, decays_ref,
+):
+    decays_ref[...] = joined_decay(recv_ref[SOON * HD :, :])
     total_ref[...] = lifted_heads(
-        groups, core == 1, decays, recv_ref, projc_ref[:, HD:], a_ref, g_ref,
-        jnp.zeros((ROWS, HD), F32), keep,
+        (own_ref, fa_ref, fb_ref), order_of(my_core())[:SOON], recv_ref, decays_ref,
+        projc_ref[:, HD:], a_ref, g_ref, gated_ref, jnp.zeros((ROWS, HD), F32),
     )
 
 
 def last_gated_kernel(
-    projc_ref, recv_ref, ha_ref, hb_ref, a_ref, g_ref, gated_in, total_ref,
-    gated_ref, squares_ref, decays,
+    projc_ref, rest_ref, decays_ref, ha_ref, hb_ref, a_ref, g_ref, gated_in, total_ref,
+    gated_ref, squares_ref,
 ):
     del gated_in
-    core = my_core()
-    k = my_slice()
-    decays[...] = joined_decay(recv_ref[COLS:, :])
-
-    def keep(h, gated):
-        gated_ref[h] = gated
-
-    groups = (
-        (ha_ref, 4 * lax.bitwise_xor(k, 3 - 2 * core), 4),
-        (hb_ref, 4 * lax.bitwise_xor(k, 2) + 2 - 2 * core, 2),
-    )
     total = lifted_heads(
-        groups, core == 1, decays, recv_ref, projc_ref[:, HD:], a_ref, g_ref,
-        total_ref[...], keep,
+        (ha_ref, hb_ref), order_of(my_core())[SOON:], rest_ref, decays_ref,
+        projc_ref[:, HD:], a_ref, g_ref, gated_ref, total_ref[...],
     )
     squares_ref[...] = jnp.broadcast_to(
         jnp.sum(total.T, axis=0, keepdims=True), (8, ROWS)
@@ -486,15 +486,21 @@
     f32 = functools.partial(shaped, dtype=F32)
 
     params = [f32(TAPS, COLS), f32(1, COLS), f32(TAPS, 256), f32(1, 256)]
-    edge, docv, feat, proj, *params, raw = call(
+    edge, docv, feat, proj, *params, raw, bias, speed = call(
         edge_kernel, "edge",
         [
             shaped(16, PACK), shaped(8, HD, dtype=jnp.int32), shaped(ROWS, COLS),
-            shaped(ROWS, 256), *params, f32(HEADS, ROWS),
+            shaped(ROWS, 256), *params, f32(HEADS, ROWS), f32(HEADS, HD), f32(HEADS, HD),
         ],
-        (doc_offset, feat_in, state_proj, feat_taps, fbias, proj_taps, pbias, step_raw),
-        far=range(8),
-        scratch=[pltpu.SMEM((ROWS,), jnp.int32), DMA((8,))],
+        (
+            doc_offset, feat_in, state_proj, feat_taps, fbias, proj_taps, pbias, step_raw,
+            step_bias, decay_log,
+        ),
+        far=range(10),
+        scratch=[
+            pltpu.SMEM((ROWS,), jnp.int32), pltpu.SMEM((HEADS,), F32),
+            pltpu.SMEM((HEADS,), F32), DMA((11,)),
+        ],
     )
     rim = lax.ppermute(edge, "ctx", NEXT)
 
@@ -504,13 +510,14 @@
             shaped(ROWS, COLS), shaped(ROWS, 256), f32(HEADS, ROWS), f32(HEADS, ROWS),
             f32(HEADS, ROWS), f32(HEADS, HD),
         ],
-        (docv, feat, proj, *params, raw, step_bias, decay_log),
-        far=(8, 9),
-        scratch=[pltpu.SMEM((HEADS,), F32), pltpu.SMEM((HEADS,), F32), DMA((2,))],
-    )
-    featc, projc, keep, send = call(
+        (docv, feat, proj, *params, raw, bias, speed),
+    )
+    featc, projc, keep, send, rest = call(
         state_kernel, "state",
-        [shaped(ROWS, COLS), shaped(ROWS, 256), f32(COLS, HD), shaped(COLS + 32, HD)],
+        [
+            shaped(ROWS, COLS), shaped(ROWS, 256), f32(COLS, HD), shaped(SOON * HD + 32, HD),
+            shaped((HEADS - SOON) * HD, HD),
+        ],
         (docv, rim, feat, proj, *params, coef, decay, featc, projc),
         scratch=[pltpu.VMEM((32, COLS + 256), F32)],
         aliases={10: 0, 11: 1},
@@ -547,7 +554,10 @@
         (own, own_decay, ra, ga, rb, gb),
     )
     q = lax.ppermute(total, "ctx", LATER)
+    rest, chips = lax.optimization_barrier((rest, chips))
+    rest = lax.ppermute(rest, "ctx", CORE)
     other = lax.ppermute(q, "ctx", CORE)
+    other, rest = lax.optimization_barrier((other, rest))
     e_own, ea, eb = call(
         enter_kernel, "enter",
         [f32(QUARTER, HD), shaped(QUARTER, HD), shaped(2 * HD, HD)],
@@ -558,15 +568,14 @@
     fa = lax.ppermute(ea, "ctx", APART)
     ha = lax.ppermute(fa, "ctx", CORE)
     hb = lax.ppermute(fb, "ctx", CORE)
-    gated, squares = call(
-        gated_kernel, "gated", [f32(HEADS, ROWS, HD), f32(ROWS, HD)],
-        (projc, recv, e_own, fa, fb, a, g), scratch=[pltpu.VMEM((HEADS, HD), F32)],
+    gated, squares, early_decay = call(
+        gated_kernel, "gated", [f32(HEADS, ROWS, HD), f32(ROWS, HD), f32(HEADS, HD)],
+        (projc, recv, e_own, fa, fb, a, g),
     )
     gated, squares = call(
         last_gated_kernel, "last_gated", [f32(HEADS, ROWS, HD), f32(8, ROWS)],
-        (projc, recv, ha, hb, a, g, gated, squares),
-        scratch=[pltpu.VMEM((HEADS, HD), F32)],
-        aliases={6: 0},
+        (projc, rest, early_decay, ha, hb, a, g, gated, squares),
+        aliases={7: 0},
     )
     s2 = lax.ppermute(squares, "head", HEAD_XOR[2])
     s3 = lax.ppermute(squares, "head", HEAD_XOR[3])

time: 56.5 us -> 54.6 us (0.966)
  starting transfers between devices: 20.4 us -> 17.2 us
  waiting for transfers between devices: 25.4 us -> 27.7 us
  Pallas kernels: 10.4 us -> 9.41 us
    ppermute x1, waiting for transfers between devices: 0.17 us -> 2.89 us  [body(): rb = lax.ppermute(tb, 'ctx', TWO)]
    ppermute x1, starting transfers between devices: 2.15 us -> 0.09 us  [body(): fa = lax.ppermute(ea, 'ctx', APART)]
    ppermute x1, starting transfers between devices: 1.22 us -> 2.73 us  [body(): fb = lax.ppermute(eb, 'ctx', TWO)]
    ppermute x1, waiting for transfers between devices: 2.66 us -> 4.02 us  [body(): fa = lax.ppermute(ea, 'ctx', APART)]
    ppermute x1, starting transfers between devices: 1.32 us -> 0.17 us  [body(): ha = lax.ppermute(fa, 'ctx', CORE)]
    ppermute x1, waiting for transfers between devices: 2.54 us -> 1.41 us  [body(): fb = lax.ppermute(eb, 'ctx', TWO)]
    ppermute x1, waiting for transfers between devices: 4.31 us -> 5.43 us  [body(): rim = lax.ppermute(edge, 'ctx', NEXT)]
    ppermute x1, starting transfers between devices: 3.73 us -> 2.62 us  [body(): rb = lax.ppermute(tb, 'ctx', TWO)]
  transfers between devices with their start and end apart: 15 -> 16, of which waited for: 12 -> 11; matrix products, arithmetic and copies ran while one was open for 0% -> 0% of each run, Pallas kernels for 11% -> 9%
where the time goes in v2:
time: 54.6 us; the launch traced here: 54.4 us
  waiting for transfers between devices  27.7 us (51%)
  starting transfers between devices  17.2 us (32%)
  Pallas kernels  9.41 us (17%)
    pallas_call x10, Pallas kernels, call(): pl.pallas_call(kernel, name=name, out_shape=out, in_specs=[HBM if i in fa...  9.41 us
    ppermute x1, waiting for transfers between devices, body(): q = lax.ppermute(total, 'ctx', LATER)  5.59 us
    ppermute x1, waiting for transfers between devices, body(): rim = lax.ppermute(edge, 'ctx', NEXT)  5.43 us
    ppermute x1, starting transfers between devices, body(): q = lax.ppermute(total, 'ctx', LATER)  4.22 us
    ppermute x1, waiting for transfers between devices, body(): fa = lax.ppermute(ea, 'ctx', APART)  4.02 us
    ppermute x1, starting transfers between devices, body(): s2 = lax.ppermute(squares, 'head', HEAD_XOR[2])  3.29 us
    ppermute x1, waiting for transfers between devices, body(): s3 = lax.ppermute(squares, 'head', HEAD_XOR[3])  2.91 us
    ppermute x1, waiting for transfers between devices, body(): rb = lax.ppermute(tb, 'ctx', TWO)  2.89 us
  transfers between devices with their start and end apart: 16, of which 11 were waited for; matrix products, arithmetic and copies ran while one was open for 0% of the time, Pallas kernels for 9%

profile of v2, /device:TPU:6, one launch (start us, length us, event | category | flops | bytes accessed | tf_op | source)
XLA Modules:
  0.0 54.4 jit_solution(5063597931875473985)
XLA Ops:
  0.0 1.5 %edge.1 = (bf16[16,640]{1,0:T(8,128)(2,1)S(1)}, s32[8,128]{1,0:T(8,128)S(1)}, bf16[256,2048]{1,0:T(8,128)(2,1)S(1)}, bf16[256,256]{1,0:T(8,128)(2,1)S(1)}, f32[4...) custom-call(s32[256]{0:T(256)} %doc_hbm.1, ...), custom_call_target="tpu_custom_call" | custom-call | tf_op jit(solution)/shard_map/edge/pallas_call | solution.py:467
  1.5 1.9 %collective-permute-start = (bf16[16,640]{1,0:T(8,128)(2,1)S(1)}, bf16[16,640]{1,0:T(8,128)(2,1)S(1)}, u32[]{:S(2)}, u32[]{:S(2)}) collective-permute-start(bf16[16,640]{1,0:T(8,128)(2,1)S(1)} %get-tuple-element.55), channel_id=1, source_target_pairs={{0,4},{4,8},{8,12},{12,16},{16,20},{20,24},{24,28},{28,32},{32,36}... | collective-permute-start | bytes 61448 | tf_op jit(solution)/shard_map/ppermute | solution.py:505
  3.4 1.6 %conv.1 = (bf16[256,2048]{1,0:T(8,128)(2,1)S(1)}, bf16[256,256]{1,0:T(8,128)(2,1)S(1)}, f32[16,256]{1,0:T(8,128)S(1)}, f32[16,256]{1,0:T(8,128)S(1)}, f32[16,256]{1,0:T(8,128)S(1)}, /*index=5*/f32[16,128]{1,0:T(8,128)S(1)}) custom-call(s32[8,128]{1,0:T(8,128)S(1)} %get-tuple-element.54.docv_ref, bf16[256,2048]{1,0:T(8,128)(2,1)S(1)} %get-tuple-element.56.feat_ref, ...), custom_call_target="tpu_custom_call" | custom-call | tf_op jit(solution)/shard_map/conv/pallas_call | solution.py:467
  5.0 5.4 %collective-permute-done.rim_ref = bf16[16,640]{1,0:T(8,128)(2,1)S(1)} collective-permute-done((bf16[16,640]{1,0:T(8,128)(2,1)S(1)}, bf16[16,640]{1,0:T(8,128)(2,1)S(1)}, u32[]{:S(2)}, u32[]{:S(2)}) %collective-permute-start) | collective-permute-done | bytes 20512 | tf_op jit(solution)/shard_map/ppermute | solution.py:505
  10.4 0.6 %state.1 = (bf16[256,2048]{1,0:T(8,128)(2,1)S(1)}, bf16[256,256]{1,0:T(8,128)(2,1)S(1)}, f32[2048,128]{1,0:T(8,128)S(1)}, bf16[1312,128]{1,0:T(8,128)(2,1)S(1)}, bf16[768,128]{1,0:T(8,128)(2,1)S(1)}) custom-call(s32[8,128]{1,0:T(8,128)S(1)} %get-tuple-element.54.docv_ref, ...), custom_call_target="tpu_custom_call", output_to_operand_aliasing={{0}: (10, {}), {1}: (11, {})} | custom-call | tf_op jit(solution)/shard_map/state/pallas_call | solution.py:467
  11.1 1.6 %collective-permute-done.1.recv_ref = bf16[1312,128]{1,0:T(8,128)(2,1)S(1)} collective-permute-done((bf16[1312,128]{1,0:T(8,128)(2,1)S(1)}, bf16[1312,128]{1,0:T(8,128)(2,1)S(1)}, u32[]{:S(2)}, u32[]{:S(2)}) %collective-permute-start.1) | collective-permute-done | bytes 335904 | tf_op jit(solution)/shard_map/ppermute | solution.py:525
  13.0 2.6 %collective-permute-start.3 = (bf16[272,128]{1,0:T(8,128)(2,1)S(1)}, bf16[272,128]{1,0:T(8,128)(2,1)S(1)}, u32[]{:S(2)}, u32[]{:S(2)}) collective-permute-start(bf16[272,128]{1,0:T(8,128)(2,1)S(1)} %get-tuple-element.77), channel_id=1, source_target_pairs={{0,16},{4,20},{8,24},{12,28},{16,0},{20,4},{24,8},{28,12},{32,48},... | collective-permute-start | bytes 208904 | tf_op jit(solution)/shard_map/ppermute | solution.py:533
  15.6 2.9 %inner.1 = (f32[16,256,128]{2,1,0:T(8,128)S(1)}, f32[16,256,128]{2,1,0:T(8,128)S(1)}, f32[1,2048]{1,0:T(1,128)S(1)}) custom-call(s32[8,128]{1,0:T(8,128)S(1)} %get-tuple-element.54.docv_ref, bf16[256,2048]{1,0:T(8,128)(2,1)S(1)} %get-tuple-element.78.featc_ref, bf16[256,256]{1,0:T(8,128)(2,1)S(1)} %get-tuple-element.74.projc_ref, ...), custom_call_target="tpu_custom_call" | custom-call | tf_op jit(solution)/shard_map/inner/pallas_call | solution.py:467
  18.5 2.9 %collective-permute-done.3.rb_ref = bf16[272,128]{1,0:T(8,128)(2,1)S(1)} collective-permute-done((bf16[272,128]{1,0:T(8,128)(2,1)S(1)}, bf16[272,128]{1,0:T(8,128)(2,1)S(1)}, u32[]{:S(2)}, u32[]{:S(2)}) %collective-permute-start.3) | collective-permute-done | bytes 69664 | tf_op jit(solution)/shard_map/ppermute | solution.py:533
  21.9 1.2 %collective-permute-done.5.gb_ref = bf16[272,128]{1,0:T(8,128)(2,1)S(1)} collective-permute-done((bf16[272,128]{1,0:T(8,128)(2,1)S(1)}, bf16[272,128]{1,0:T(8,128)(2,1)S(1)}, u32[]{:S(2)}, u32[]{:S(2)}) %collective-permute-start.5) | collective-permute-done | bytes 69664 | tf_op jit(solution)/shard_map/ppermute | solution.py:550
  23.3 4.2 %collective-permute-start.6 = (bf16[528,128]{1,0:T(8,128)(2,1)S(1)}, bf16[528,128]{1,0:T(8,128)(2,1)S(1)}, u32[]{:S(2)}, u32[]{:S(2)}) collective-permute-start(bf16[528,128]{1,0:T(8,128)(2,1)S(1)} %get-tuple-element.84), channel_id=1, source_target_pairs={{0,48},{4,68},{8,56},{12,76},{16,32},{20,84},{24,40},{28,92},{32,8... | collective-permute-start | bytes 405512 | tf_op jit(solution)/shard_map/ppermute | solution.py:556
  27.6 5.6 %collective-permute-done.6.q_ref = bf16[528,128]{1,0:T(8,128)(2,1)S(1)} collective-permute-done((bf16[528,128]{1,0:T(8,128)(2,1)S(1)}, bf16[528,128]{1,0:T(8,128)(2,1)S(1)}, u32[]{:S(2)}, u32[]{:S(2)}) %collective-permute-start.6) | collective-permute-done | bytes 135200 | tf_op jit(solution)/shard_map/ppermute | solution.py:556
  33.2 1.3 %collective-permute-done.7.other_ref = bf16[528,128]{1,0:T(8,128)(2,1)S(1)} collective-permute-done((bf16[528,128]{1,0:T(8,128)(2,1)S(1)}, bf16[528,128]{1,0:T(8,128)(2,1)S(1)}, u32[]{:S(2)}, u32[]{:S(2)}) %collective-permute-start.7) | collective-permute-done | bytes 135200 | tf_op jit(solution)/shard_map/ppermute | solution.py:559
  34.8 2.7 %collective-permute-start.10 = (bf16[256,128]{1,0:T(8,128)(2,1)S(1)}, bf16[256,128]{1,0:T(8,128)(2,1)S(1)}, u32[]{:S(2)}, u32[]{:S(2)}) collective-permute-start(bf16[256,128]{1,0:T(8,128)(2,1)S(1)} %get-tuple-element.94), channel_id=1, source_target_pairs={{0,16},{4,20},{8,24},{12,28},{16,0},{20,4},{24,8},{28,12},{32,48},... | collective-permute-start | bytes 196616 | tf_op jit(solution)/shard_map/ppermute | solution.py:567
  37.6 4.0 %collective-permute-done.9.fa_ref = bf16[512,128]{1,0:T(8,128)(2,1)S(1)} collective-permute-done((bf16[512,128]{1,0:T(8,128)(2,1)S(1)}, bf16[512,128]{1,0:T(8,128)(2,1)S(1)}, u32[]{:S(2)}, u32[]{:S(2)}) %collective-permute-start.9) | collective-permute-done | bytes 131104 | tf_op jit(solution)/shard_map/ppermute | solution.py:568
  41.8 1.4 %collective-permute-done.10.fb_ref = bf16[256,128]{1,0:T(8,128)(2,1)S(1)} collective-permute-done((bf16[256,128]{1,0:T(8,128)(2,1)S(1)}, bf16[256,128]{1,0:T(8,128)(2,1)S(1)}, u32[]{:S(2)}, u32[]{:S(2)}) %collective-permute-start.10) | collective-permute-done | bytes 65568 | tf_op jit(solution)/shard_map/ppermute | solution.py:567
  43.5 0.5 gated.1
  44.0 0.4 collective-permute-done.12.hb_ref
  44.4 0.5 last_gated.1
  44.9 3.3 %collective-permute-start.15 = (f32[8,256]{1,0:T(8,128)S(1)}, f32[8,256]{1,0:T(8,128)S(1)}, u32[]{:S(2)}, u32[]{:S(2)}) collective-permute-start(f32[8,256]{1,0:T(8,128)S(1)} %get-tuple-element.101.s0), channel_id=1, source_target_pairs={{0,2},{1,3},{2,0},{3,1},{4,6},{5,7},{6,4},{7,5},{8,10},{9,11},{10,... | collective-permute-start | bytes 24584 | tf_op jit(solution)/shard_map/ppermute | solution.py:580
  48.2 1.0 %collective-permute-start.14 = (f32[8,256]{1,0:T(8,128)S(1)}, f32[8,256]{1,0:T(8,128)S(1)}, u32[]{:S(2)}, u32[]{:S(2)}) collective-permute-start(f32[8,256]{1,0:T(8,128)S(1)} %get-tuple-element.101.s0), channel_id=1, source_target_pairs={{0,3},{1,2},{2,1},{3,0},{4,7},{5,6},{6,5},{7,4},{8,11},{9,10},{10,... | collective-permute-start | bytes 24584 | tf_op jit(solution)/shard_map/ppermute | solution.py:581
  49.3 0.9 %collective-permute-done.15.s2 = f32[8,256]{1,0:T(8,128)S(1)} collective-permute-done((f32[8,256]{1,0:T(8,128)S(1)}, f32[8,256]{1,0:T(8,128)S(1)}, u32[]{:S(2)}, u32[]{:S(2)}) %collective-permute-start.15) | collective-permute-done | bytes 8224 | tf_op jit(solution)/shard_map/ppermute | solution.py:580
  50.2 2.9 %collective-permute-done.14.s3 = f32[8,256]{1,0:T(8,128)S(1)} collective-permute-done((f32[8,256]{1,0:T(8,128)S(1)}, f32[8,256]{1,0:T(8,128)S(1)}, u32[]{:S(2)}, u32[]{:S(2)}) %collective-permute-start.14) | collective-permute-done | bytes 8224 | tf_op jit(solution)/shard_map/ppermute | solution.py:581
  53.1 1.3 %norm.1 = bf16[256,2048]{1,0:T(8,128)(2,1)} custom-call(f32[16,256,128]{2,1,0:T(8,128)S(1)} %get-tuple-element.100.gated_ref, f32[8,256]{1,0:T(8,128)S(1)} %get-tuple-element.101.s0, f32[8,256]{1,0:T(8,128)S(1)} %collective-permute-done.13.s1, f32[8,256]{1,0:T(8,128)S(1)} %collective-permute-done.14.s3, f32[8,256]{1,0:T(8,128)S(1)} %collective-permute-done.15.s2, ...), custom_call_target="tpu_custom_call" | custom-call | tf_op jit(solution)/shard_map/norm/pallas_call | solution.py:467
  (18 shorter events, 1.9 us)
Async XLA Ops:
  1.5 8.9 %collective-permute-start = (bf16[16,640]{1,0:T(8,128)(2,1)S(1)}, bf16[16,640]{1,0:T(8,128)(2,1)S(1)}, u32[]{:S(2)}, u32[]{:S(2)}) collective-permute-start(bf16[16,640]{1,0:T(8,128)(2,1)S(1)} %get-tuple-element.55), channel_id=1, source_target_pairs={{0,4},{4,8},{8,12},{12,16},{16,20},{20,24},{24,28},{28,32},{32,36}... | collective-permute-start | bytes 61448 | tf_op jit(solution)/shard_map/ppermute | solution.py:505
  11.0 1.7 %collective-permute-start.1 = (bf16[1312,128]{1,0:T(8,128)(2,1)S(1)}, bf16[1312,128]{1,0:T(8,128)(2,1)S(1)}, u32[]{:S(2)}, u32[]{:S(2)}) collective-permute-start(bf16[1312,128]{1,0:T(8,128)(2,1)S(1)} %get-tuple-element.72), channel_id=1, source_target_pairs={{0,4},{4,0},{8,12},{12,8},{16,20},{20,16},{24,28},{28,24},{32,36},... | collective-permute-start | bytes 1007624 | tf_op jit(solution)/shard_map/ppermute | solution.py:525
  12.9 8.5 %collective-permute-start.2 = (bf16[528,128]{1,0:T(8,128)(2,1)S(1)}, bf16[528,128]{1,0:T(8,128)(2,1)S(1)}, u32[]{:S(2)}, u32[]{:S(2)}) collective-permute-start(bf16[528,128]{1,0:T(8,128)(2,1)S(1)} %get-tuple-element.73), channel_id=1, source_target_pairs={{0,8},{4,28},{8,0},{12,20},{16,24},{20,12},{24,16},{28,4},{32,40},... | collective-permute-start | bytes 405512 | tf_op jit(solution)/shard_map/ppermute | solution.py:534
  13.0 8.4 %collective-permute-start.3 = (bf16[272,128]{1,0:T(8,128)(2,1)S(1)}, bf16[272,128]{1,0:T(8,128)(2,1)S(1)}, u32[]{:S(2)}, u32[]{:S(2)}) collective-permute-start(bf16[272,128]{1,0:T(8,128)(2,1)S(1)} %get-tuple-element.77), channel_id=1, source_target_pairs={{0,16},{4,20},{8,24},{12,28},{16,0},{20,4},{24,8},{28,12},{32,48},... | collective-permute-start | bytes 208904 | tf_op jit(solution)/shard_map/ppermute | solution.py:533
  21.4 1.7 %collective-permute-start.4 = (bf16[528,128]{1,0:T(8,128)(2,1)S(1)}, bf16[528,128]{1,0:T(8,128)(2,1)S(1)}, u32[]{:S(2)}, u32[]{:S(2)}) collective-permute-start(bf16[528,128]{1,0:T(8,128)(2,1)S(1)} %collective-permute-done.2.ra_ref), channel_id=1, source_target_pairs={{0,4},{4,0},{8,12},{12,8},{16,20},{20,16},{24,28},{28,24},{32,36},... | collective-permute-start | bytes 405512 | tf_op jit(solution)/shard_map/ppermute | solution.py:549
  21.8 1.3 %collective-permute-start.5 = (bf16[272,128]{1,0:T(8,128)(2,1)S(1)}, bf16[272,128]{1,0:T(8,128)(2,1)S(1)}, u32[]{:S(2)}, u32[]{:S(2)}) collective-permute-start(bf16[272,128]{1,0:T(8,128)(2,1)S(1)} %collective-permute-done.3.rb_ref), channel_id=1, source_target_pairs={{0,4},{4,0},{8,12},{12,8},{16,20},{20,16},{24,28},{28,24},{32,36},... | collective-permute-start | bytes 208904 | tf_op jit(solution)/shard_map/ppermute | solution.py:550
  23.3 9.9 %collective-permute-start.6 = (bf16[528,128]{1,0:T(8,128)(2,1)S(1)}, bf16[528,128]{1,0:T(8,128)(2,1)S(1)}, u32[]{:S(2)}, u32[]{:S(2)}) collective-permute-start(bf16[528,128]{1,0:T(8,128)(2,1)S(1)} %get-tuple-element.84), channel_id=1, source_target_pairs={{0,48},{4,68},{8,56},{12,76},{16,32},{20,84},{24,40},{28,92},{32,8... | collective-permute-start | bytes 405512 | tf_op jit(solution)/shard_map/ppermute | solution.py:556
  27.5 5.7 %collective-permute-start.8 = (bf16[768,128]{1,0:T(8,128)(2,1)S(1)}, bf16[768,128]{1,0:T(8,128)(2,1)S(1)}, u32[]{:S(2)}, u32[]{:S(2)}) collective-permute-start(bf16[768,128]{1,0:T(8,128)(2,1)S(1)} %get-tuple-element.87), channel_id=1, source_target_pairs={{0,4},{4,0},{8,12},{12,8},{16,20},{20,16},{24,28},{28,24},{32,36},... | collective-permute-start | bytes 589832 | tf_op jit(solution)/shard_map/ppermute | solution.py:558
  33.2 1.4 %collective-permute-start.7 = (bf16[528,128]{1,0:T(8,128)(2,1)S(1)}, bf16[528,128]{1,0:T(8,128)(2,1)S(1)}, u32[]{:S(2)}, u32[]{:S(2)}) collective-permute-start(bf16[528,128]{1,0:T(8,128)(2,1)S(1)} %collective-permute-done.6.q_ref), channel_id=1, source_target_pairs={{0,4},{4,0},{8,12},{12,8},{16,20},{20,16},{24,28},{28,24},{32,36},... | collective-permute-start | bytes 405512 | tf_op jit(solution)/shard_map/ppermute | solution.py:559
  34.7 6.8 %collective-permute-start.9 = (bf16[512,128]{1,0:T(8,128)(2,1)S(1)}, bf16[512,128]{1,0:T(8,128)(2,1)S(1)}, u32[]{:S(2)}, u32[]{:S(2)}) collective-permute-start(bf16[512,128]{1,0:T(8,128)(2,1)S(1)} %get-tuple-element.93), channel_id=1, source_target_pairs={{0,8},{4,28},{8,0},{12,20},{16,24},{20,12},{24,16},{28,4},{32,40},... | collective-permute-start | bytes 393224 | tf_op jit(solution)/shard_map/ppermute | solution.py:568
  34.8 8.3 %collective-permute-start.10 = (bf16[256,128]{1,0:T(8,128)(2,1)S(1)}, bf16[256,128]{1,0:T(8,128)(2,1)S(1)}, u32[]{:S(2)}, u32[]{:S(2)}) collective-permute-start(bf16[256,128]{1,0:T(8,128)(2,1)S(1)} %get-tuple-element.94), channel_id=1, source_target_pairs={{0,16},{4,20},{8,24},{12,28},{16,0},{20,4},{24,8},{28,12},{32,48},... | collective-permute-start | bytes 196616 | tf_op jit(solution)/shard_map/ppermute | solution.py:567
  41.6 2.8 %collective-permute-start.11 = (bf16[512,128]{1,0:T(8,128)(2,1)S(1)}, bf16[512,128]{1,0:T(8,128)(2,1)S(1)}, u32[]{:S(2)}, u32[]{:S(2)}) collective-permute-start(bf16[512,128]{1,0:T(8,128)(2,1)S(1)} %collective-permute-done.9.fa_ref), channel_id=1, source_target_pairs={{0,4},{4,0},{8,12},{12,8},{16,20},{20,16},{24,28},{28,24},{32,36},... | collective-permute-start | bytes 393224 | tf_op jit(solution)/shard_map/ppermute | solution.py:569
  43.2 1.3 %collective-permute-start.12 = (bf16[256,128]{1,0:T(8,128)(2,1)S(1)}, bf16[256,128]{1,0:T(8,128)(2,1)S(1)}, u32[]{:S(2)}, u32[]{:S(2)}) collective-permute-start(bf16[256,128]{1,0:T(8,128)(2,1)S(1)} %collective-permute-done.10.fb_ref), channel_id=1, source_target_pairs={{0,4},{4,0},{8,12},{12,8},{16,20},{20,16},{24,28},{28,24},{32,36},... | collective-permute-start | bytes 196616 | tf_op jit(solution)/shard_map/ppermute | solution.py:570
  44.9 5.2 %collective-permute-start.15 = (f32[8,256]{1,0:T(8,128)S(1)}, f32[8,256]{1,0:T(8,128)S(1)}, u32[]{:S(2)}, u32[]{:S(2)}) collective-permute-start(f32[8,256]{1,0:T(8,128)S(1)} %get-tuple-element.101.s0), channel_id=1, source_target_pairs={{0,2},{1,3},{2,0},{3,1},{4,6},{5,7},{6,4},{7,5},{8,10},{9,11},{10,... | collective-permute-start | bytes 24584 | tf_op jit(solution)/shard_map/ppermute | solution.py:580
  48.2 4.9 %collective-permute-start.14 = (f32[8,256]{1,0:T(8,128)S(1)}, f32[8,256]{1,0:T(8,128)S(1)}, u32[]{:S(2)}, u32[]{:S(2)}) collective-permute-start(f32[8,256]{1,0:T(8,128)S(1)} %get-tuple-element.101.s0), channel_id=1, source_target_pairs={{0,3},{1,2},{2,1},{3,0},{4,7},{5,6},{6,5},{7,4},{8,11},{9,10},{10,... | collective-permute-start | bytes 24584 | tf_op jit(solution)/shard_map/ppermute | solution.py:581
  49.3 3.8 %collective-permute-start.13 = (f32[8,256]{1,0:T(8,128)S(1)}, f32[8,256]{1,0:T(8,128)S(1)}, u32[]{:S(2)}, u32[]{:S(2)}) collective-permute-start(f32[8,256]{1,0:T(8,128)S(1)} %get-tuple-element.101.s0), channel_id=1, source_target_pairs={{0,1},{1,0},{2,3},{3,2},{4,5},{5,4},{6,7},{7,6},{8,9},{9,8},{10,11... | collective-permute-start | bytes 24584 | tf_op jit(solution)/shard_map/ppermute | solution.py:582

commit v3 on v2

--- a/solution.py
+++ b/solution.py
@@ -385,7 +385,7 @@
             a_ref[h, top : top + HD, :] = (inner + skip_ref[h] * feat) * gate[top : top + HD]
 
 
-def lifted_heads(refs, heads, early_ref, decays, c, a_ref, g_ref, gated_ref, total):
+def lifted_heads(refs, heads, early_ref, decays, c, a_ref, g_ref, gain_ref, gated_ref, total):
     second = my_core() == 1
     states = [
         ref[i * HD : (i + 1) * HD, :] for ref in refs for i in range(ref.shape[0] // HD)
@@ -400,48 +400,49 @@
             c, low, preferred_element_type=F32
         )
         gated = a_ref[h] + lifted * g_ref[h]
-        gated_ref[h] = gated
+        cols = pl.ds(pl.multiple_of(h * HD, HD), HD)
+        gated_ref[h] = gated * gain_ref[0:1, cols]
         total = total + gated * gated
     return total
 
 
 def gated_kernel(
-    projc_ref, recv_ref, own_ref, fa_ref, fb_ref, a_ref, g_ref,
+    projc_ref, recv_ref, own_ref, fa_ref, fb_ref, a_ref, g_ref, gain_ref,
     gated_ref, total_ref, decays_ref,
 ):
     decays_ref[...] = joined_decay(recv_ref[SOON * HD :, :])
     total_ref[...] = lifted_heads(
         (own_ref, fa_ref, fb_ref), order_of(my_core())[:SOON], recv_ref, decays_ref,
-        projc_ref[:, HD:], a_ref, g_ref, gated_ref, jnp.zeros((ROWS, HD), F32),
+        projc_ref[:, HD:], a_ref, g_ref, gain_ref, gated_ref, jnp.zeros((ROWS, HD), F32),
     )
 
 
 def last_gated_kernel(
-    projc_ref, rest_ref, decays_ref, ha_ref, hb_ref, a_ref, g_ref, gated_in, total_ref,
+    projc_ref, rest_ref, decays_ref, ha_ref, hb_ref, a_ref, g_ref, gain_ref, gated_in, total_ref,
     gated_ref, squares_ref,
 ):
     del gated_in
     total = lifted_heads(
         (ha_ref, hb_ref), order_of(my_core())[SOON:], rest_ref, decays_ref,
-        projc_ref[:, HD:], a_ref, g_ref, gated_ref, total_ref[...],
+        projc_ref[:, HD:], a_ref, g_ref, gain_ref, gated_ref, total_ref[...],
     )
     squares_ref[...] = jnp.broadcast_to(
         jnp.sum(total.T, axis=0, keepdims=True), (8, ROWS)
     )
 
 
-def norm_kernel(gated_ref, s0, s1, s3, s2, gain_ref, out_hbm, out_ref, sems):
+def norm_kernel(gated_ref, s0, s1, s3, s2, out_hbm, out_ref, sems):
     total = (s0[0:1] + s1[0:1]) + (s2[0:1] + s3[0:1])
     scale = lax.rsqrt(total / (COLS * YS) + 1e-05)
     scale = jnp.broadcast_to(scale, (HD, ROWS)).T
     copies = []
     for i in range(HEADS):
         cols = slice(i * HD, (i + 1) * HD)
-        out_ref[:, cols] = (gated_ref[i] * scale * gain_ref[0:1, cols]).astype(BF16)
-        if i % 4 == 3:
-            cols = pl.ds((i - 3) * HD, 4 * HD)
+        out_ref[:, cols] = (gated_ref[i] * scale).astype(BF16)
+        if i % 2 == 1:
+            cols = pl.ds((i - 1) * HD, 2 * HD)
             copy = pltpu.make_async_copy(
-                out_ref.at[:, cols], out_hbm.at[:, cols], sems.at[i // 4]
+                out_ref.at[:, cols], out_hbm.at[:, cols], sems.at[i // 2]
             )
             copy.start()
             copies.append(copy)
@@ -545,7 +546,7 @@
             DMA((3,)),
         ],
     )
-    ra, rb, a = lax.optimization_barrier((ra, rb, a))
+    ra, a = lax.optimization_barrier((ra, a))
     ga = lax.ppermute(ra, "ctx", CORE)
     gb = lax.ppermute(rb, "ctx", CORE)
     total, chips, decays = call(
@@ -570,19 +571,19 @@
     hb = lax.ppermute(fb, "ctx", CORE)
     gated, squares, early_decay = call(
         gated_kernel, "gated", [f32(HEADS, ROWS, HD), f32(ROWS, HD), f32(HEADS, HD)],
-        (projc, recv, e_own, fa, fb, a, g),
+        (projc, recv, e_own, fa, fb, a, g, gain),
     )
     gated, squares = call(
         last_gated_kernel, "last_gated", [f32(HEADS, ROWS, HD), f32(8, ROWS)],
-        (projc, rest, early_decay, ha, hb, a, g, gated, squares),
-        aliases={7: 0},
+        (projc, rest, early_decay, ha, hb, a, g, gain, gated, squares),
+        aliases={8: 0},
     )
     s2 = lax.ppermute(squares, "head", HEAD_XOR[2])
     s3 = lax.ppermute(squares, "head", HEAD_XOR[3])
     s1 = lax.ppermute(squares, "head", HEAD_XOR[1])
     return call(
-        norm_kernel, "norm", shaped(ROWS, COLS), (gated, squares, s1, s3, s2, gain),
-        scratch=[pltpu.VMEM((ROWS, COLS), BF16), DMA((HEADS // 4,))],
+        norm_kernel, "norm", shaped(ROWS, COLS), (gated, squares, s1, s3, s2),
+        scratch=[pltpu.VMEM((ROWS, COLS), BF16), DMA((HEADS // 2,))],
         out_specs=HBM,
     )
 

time: 54.6 us -> 54.1 us (level)
  waiting for transfers between devices: 27.7 us -> 26.8 us
    ppermute x1, waiting for transfers between devices: 2.89 us -> 1.48 us  [body(): rb = lax.ppermute(tb, 'ctx', TWO)]
    ppermute x1, waiting for transfers between devices: 0.01 us -> 1.39 us  [body(): ra = lax.ppermute(ta, 'ctx', APART)]
  transfers between devices with their start and end apart: 16 -> 16, of which waited for: 11 -> 12; matrix products, arithmetic and copies ran while one was open for 0% -> 0% of each run, Pallas kernels for 9% -> 9%
where the time goes in v3:
time: 54.1 us; the launch traced here: 53.9 us
  waiting for transfers between devices  26.8 us (50%)
  starting transfers between devices  17.6 us (33%)
  Pallas kernels  9.4 us (17%)
    pallas_call x10, Pallas kernels, call(): pl.pallas_call(kernel, name=name, out_shape=out, in_specs=[HBM if i in fa...  9.4 us
    ppermute x1, waiting for transfers between devices, body(): rim = lax.ppermute(edge, 'ctx', NEXT)  5.43 us
    ppermute x1, waiting for transfers between devices, body(): q = lax.ppermute(total, 'ctx', LATER)  5.43 us
    ppermute x1, starting transfers between devices, body(): q = lax.ppermute(total, 'ctx', LATER)  4.38 us
    ppermute x1, waiting for transfers between devices, body(): fa = lax.ppermute(ea, 'ctx', APART)  3.94 us
    ppermute x1, starting transfers between devices, body(): s2 = lax.ppermute(squares, 'head', HEAD_XOR[2])  3.28 us
    ppermute x1, waiting for transfers between devices, body(): s3 = lax.ppermute(squares, 'head', HEAD_XOR[3])  2.9 us
    ppermute x1, starting transfers between devices, body(): fb = lax.ppermute(eb, 'ctx', TWO)  2.89 us
  transfers between devices with their start and end apart: 16, of which 12 were waited for; matrix products, arithmetic and copies ran while one was open for 0% of the time, Pallas kernels for 9%

profile of v3, /device:TPU:6, one launch (start us, length us, event | category | flops | bytes accessed | tf_op | source)
XLA Modules:
  0.0 53.9 jit_solution(14558680559965550574)
XLA Ops:
  0.0 1.5 %edge.1 = (bf16[16,640]{1,0:T(8,128)(2,1)S(1)}, s32[8,128]{1,0:T(8,128)S(1)}, bf16[256,2048]{1,0:T(8,128)(2,1)S(1)}, bf16[256,256]{1,0:T(8,128)(2,1)S(1)}, f32[4...) custom-call(s32[256]{0:T(256)} %doc_hbm.1, ...), custom_call_target="tpu_custom_call" | custom-call | tf_op jit(solution)/shard_map/edge/pallas_call | solution.py:468
  1.5 1.9 %collective-permute-start = (bf16[16,640]{1,0:T(8,128)(2,1)S(1)}, bf16[16,640]{1,0:T(8,128)(2,1)S(1)}, u32[]{:S(2)}, u32[]{:S(2)}) collective-permute-start(bf16[16,640]{1,0:T(8,128)(2,1)S(1)} %get-tuple-element.54), channel_id=1, source_target_pairs={{0,4},{4,8},{8,12},{12,16},{16,20},{20,24},{24,28},{28,32},{32,36}... | collective-permute-start | bytes 61448 | tf_op jit(solution)/shard_map/ppermute | solution.py:506
  3.4 1.6 %conv.1 = (bf16[256,2048]{1,0:T(8,128)(2,1)S(1)}, bf16[256,256]{1,0:T(8,128)(2,1)S(1)}, f32[16,256]{1,0:T(8,128)S(1)}, f32[16,256]{1,0:T(8,128)S(1)}, f32[16,256]{1,0:T(8,128)S(1)}, /*index=5*/f32[16,128]{1,0:T(8,128)S(1)}) custom-call(s32[8,128]{1,0:T(8,128)S(1)} %get-tuple-element.53.docv_ref, bf16[256,2048]{1,0:T(8,128)(2,1)S(1)} %get-tuple-element.55.feat_ref, ...), custom_call_target="tpu_custom_call" | custom-call | tf_op jit(solution)/shard_map/conv/pallas_call | solution.py:468
  5.0 5.4 %collective-permute-done.rim_ref = bf16[16,640]{1,0:T(8,128)(2,1)S(1)} collective-permute-done((bf16[16,640]{1,0:T(8,128)(2,1)S(1)}, bf16[16,640]{1,0:T(8,128)(2,1)S(1)}, u32[]{:S(2)}, u32[]{:S(2)}) %collective-permute-start) | collective-permute-done | bytes 20512 | tf_op jit(solution)/shard_map/ppermute | solution.py:506
  10.4 0.6 %state.1 = (bf16[256,2048]{1,0:T(8,128)(2,1)S(1)}, bf16[256,256]{1,0:T(8,128)(2,1)S(1)}, f32[2048,128]{1,0:T(8,128)S(1)}, bf16[1312,128]{1,0:T(8,128)(2,1)S(1)}, bf16[768,128]{1,0:T(8,128)(2,1)S(1)}) custom-call(s32[8,128]{1,0:T(8,128)S(1)} %get-tuple-element.53.docv_ref, ...), custom_call_target="tpu_custom_call", output_to_operand_aliasing={{0}: (10, {}), {1}: (11, {})} | custom-call | tf_op jit(solution)/shard_map/state/pallas_call | solution.py:468
  11.1 1.6 %collective-permute-done.1.recv_ref = bf16[1312,128]{1,0:T(8,128)(2,1)S(1)} collective-permute-done((bf16[1312,128]{1,0:T(8,128)(2,1)S(1)}, bf16[1312,128]{1,0:T(8,128)(2,1)S(1)}, u32[]{:S(2)}, u32[]{:S(2)}) %collective-permute-start.1) | collective-permute-done | bytes 335904 | tf_op jit(solution)/shard_map/ppermute | solution.py:526
  13.0 2.6 %collective-permute-start.4 = (bf16[272,128]{1,0:T(8,128)(2,1)S(1)}, bf16[272,128]{1,0:T(8,128)(2,1)S(1)}, u32[]{:S(2)}, u32[]{:S(2)}) collective-permute-start(bf16[272,128]{1,0:T(8,128)(2,1)S(1)} %get-tuple-element.81), channel_id=1, source_target_pairs={{0,16},{4,20},{8,24},{12,28},{16,0},{20,4},{24,8},{28,12},{32,48},... | collective-permute-start | bytes 208904 | tf_op jit(solution)/shard_map/ppermute | solution.py:534
  15.6 2.9 %inner.1 = (f32[16,256,128]{2,1,0:T(8,128)S(1)}, f32[16,256,128]{2,1,0:T(8,128)S(1)}, f32[1,2048]{1,0:T(1,128)S(1)}) custom-call(s32[8,128]{1,0:T(8,128)S(1)} %get-tuple-element.53.docv_ref, bf16[256,2048]{1,0:T(8,128)(2,1)S(1)} %get-tuple-element.76.featc_ref, bf16[256,256]{1,0:T(8,128)(2,1)S(1)} %get-tuple-element.73.projc_ref, ...), custom_call_target="tpu_custom_call" | custom-call | tf_op jit(solution)/shard_map/inner/pallas_call | solution.py:468
  18.5 1.4 %collective-permute-done.2.ra_ref = bf16[528,128]{1,0:T(8,128)(2,1)S(1)} collective-permute-done((bf16[528,128]{1,0:T(8,128)(2,1)S(1)}, bf16[528,128]{1,0:T(8,128)(2,1)S(1)}, u32[]{:S(2)}, u32[]{:S(2)}) %collective-permute-start.2) | collective-permute-done | bytes 135200 | tf_op jit(solution)/shard_map/ppermute | solution.py:535
  19.9 1.5 %collective-permute-done.4.rb_ref = bf16[272,128]{1,0:T(8,128)(2,1)S(1)} collective-permute-done((bf16[272,128]{1,0:T(8,128)(2,1)S(1)}, bf16[272,128]{1,0:T(8,128)(2,1)S(1)}, u32[]{:S(2)}, u32[]{:S(2)}) %collective-permute-start.4) | collective-permute-done | bytes 69664 | tf_op jit(solution)/shard_map/ppermute | solution.py:534
  21.8 0.9 %collective-permute-done.5.gb_ref = bf16[272,128]{1,0:T(8,128)(2,1)S(1)} collective-permute-done((bf16[272,128]{1,0:T(8,128)(2,1)S(1)}, bf16[272,128]{1,0:T(8,128)(2,1)S(1)}, u32[]{:S(2)}, u32[]{:S(2)}) %collective-permute-start.5) | collective-permute-done | bytes 69664 | tf_op jit(solution)/shard_map/ppermute | solution.py:551
  22.9 4.4 %collective-permute-start.6 = (bf16[528,128]{1,0:T(8,128)(2,1)S(1)}, bf16[528,128]{1,0:T(8,128)(2,1)S(1)}, u32[]{:S(2)}, u32[]{:S(2)}) collective-permute-start(bf16[528,128]{1,0:T(8,128)(2,1)S(1)} %get-tuple-element.82), channel_id=1, source_target_pairs={{0,48},{4,68},{8,56},{12,76},{16,32},{20,84},{24,40},{28,92},{32,8... | collective-permute-start | bytes 405512 | tf_op jit(solution)/shard_map/ppermute | solution.py:557
  27.4 5.4 %collective-permute-done.6.q_ref = bf16[528,128]{1,0:T(8,128)(2,1)S(1)} collective-permute-done((bf16[528,128]{1,0:T(8,128)(2,1)S(1)}, bf16[528,128]{1,0:T(8,128)(2,1)S(1)}, u32[]{:S(2)}, u32[]{:S(2)}) %collective-permute-start.6) | collective-permute-done | bytes 135200 | tf_op jit(solution)/shard_map/ppermute | solution.py:557
  32.8 1.3 %collective-permute-done.7.other_ref = bf16[528,128]{1,0:T(8,128)(2,1)S(1)} collective-permute-done((bf16[528,128]{1,0:T(8,128)(2,1)S(1)}, bf16[528,128]{1,0:T(8,128)(2,1)S(1)}, u32[]{:S(2)}, u32[]{:S(2)}) %collective-permute-start.7) | collective-permute-done | bytes 135200 | tf_op jit(solution)/shard_map/ppermute | solution.py:560
  34.5 2.9 %collective-permute-start.10 = (bf16[256,128]{1,0:T(8,128)(2,1)S(1)}, bf16[256,128]{1,0:T(8,128)(2,1)S(1)}, u32[]{:S(2)}, u32[]{:S(2)}) collective-permute-start(bf16[256,128]{1,0:T(8,128)(2,1)S(1)} %get-tuple-element.92), channel_id=1, source_target_pairs={{0,16},{4,20},{8,24},{12,28},{16,0},{20,4},{24,8},{28,12},{32,48},... | collective-permute-start | bytes 196616 | tf_op jit(solution)/shard_map/ppermute | solution.py:568
  37.4 3.9 %collective-permute-done.9.fa_ref = bf16[512,128]{1,0:T(8,128)(2,1)S(1)} collective-permute-done((bf16[512,128]{1,0:T(8,128)(2,1)S(1)}, bf16[512,128]{1,0:T(8,128)(2,1)S(1)}, u32[]{:S(2)}, u32[]{:S(2)}) %collective-permute-start.9) | collective-permute-done | bytes 131104 | tf_op jit(solution)/shard_map/ppermute | solution.py:569
  41.6 1.2 %collective-permute-done.10.fb_ref = bf16[256,128]{1,0:T(8,128)(2,1)S(1)} collective-permute-done((bf16[256,128]{1,0:T(8,128)(2,1)S(1)}, bf16[256,128]{1,0:T(8,128)(2,1)S(1)}, u32[]{:S(2)}, u32[]{:S(2)}) %collective-permute-start.10) | collective-permute-done | bytes 65568 | tf_op jit(solution)/shard_map/ppermute | solution.py:568
  43.1 0.6 %gated.1 = (f32[16,256,128]{2,1,0:T(8,128)S(1)}, f32[256,128]{1,0:T(8,128)S(1)}, f32[16,128]{1,0:T(8,128)S(1)}) custom-call(bf16[256,256]{1,0:T(8,128)(2,1)S(1)} %get-tuple-element.73.projc_ref, bf16[1312,128]{1,0:T(8,128)(2,1)S(1)} %collective-permute-done.1.recv_ref, f32[512,128]{1,0:T(8,128)S(1)} %get-tuple-element.90.own_ref, ...), custom_call_target="tpu_custom_call" | custom-call | tf_op jit(solution)/shard_map/gated/pallas_call | solution.py:468
  44.0 0.5 last_gated.1
  44.5 3.3 %collective-permute-start.15 = (f32[8,256]{1,0:T(8,128)S(1)}, f32[8,256]{1,0:T(8,128)S(1)}, u32[]{:S(2)}, u32[]{:S(2)}) collective-permute-start(f32[8,256]{1,0:T(8,128)S(1)} %get-tuple-element.100.s0), channel_id=1, source_target_pairs={{0,2},{1,3},{2,0},{3,1},{4,6},{5,7},{6,4},{7,5},{8,10},{9,11},{10,... | collective-permute-start | bytes 24584 | tf_op jit(solution)/shard_map/ppermute | solution.py:581
  47.8 1.1 %collective-permute-start.14 = (f32[8,256]{1,0:T(8,128)S(1)}, f32[8,256]{1,0:T(8,128)S(1)}, u32[]{:S(2)}, u32[]{:S(2)}) collective-permute-start(f32[8,256]{1,0:T(8,128)S(1)} %get-tuple-element.100.s0), channel_id=1, source_target_pairs={{0,3},{1,2},{2,1},{3,0},{4,7},{5,6},{6,5},{7,4},{8,11},{9,10},{10,... | collective-permute-start | bytes 24584 | tf_op jit(solution)/shard_map/ppermute | solution.py:582
  48.9 0.9 %collective-permute-done.15.s2 = f32[8,256]{1,0:T(8,128)S(1)} collective-permute-done((f32[8,256]{1,0:T(8,128)S(1)}, f32[8,256]{1,0:T(8,128)S(1)}, u32[]{:S(2)}, u32[]{:S(2)}) %collective-permute-start.15) | collective-permute-done | bytes 8224 | tf_op jit(solution)/shard_map/ppermute | solution.py:581
  49.8 2.9 %collective-permute-done.14.s3 = f32[8,256]{1,0:T(8,128)S(1)} collective-permute-done((f32[8,256]{1,0:T(8,128)S(1)}, f32[8,256]{1,0:T(8,128)S(1)}, u32[]{:S(2)}, u32[]{:S(2)}) %collective-permute-start.14) | collective-permute-done | bytes 8224 | tf_op jit(solution)/shard_map/ppermute | solution.py:582
  52.7 1.3 %norm.1 = bf16[256,2048]{1,0:T(8,128)(2,1)} custom-call(f32[16,256,128]{2,1,0:T(8,128)S(1)} %get-tuple-element.99.gated_ref, f32[8,256]{1,0:T(8,128)S(1)} %get-tuple-element.100.s0, f32[8,256]{1,0:T(8,128)S(1)} %collective-permute-done.13.s1, f32[8,256]{1,0:T(8,128)S(1)} %collective-permute-done.14.s3, f32[8,256]{1,0:T(8,128)S(1)} %collective-permute-done.15.s2), custom_call_target="tpu_custom_call" | custom-call | tf_op jit(solution)/shard_map/norm/pallas_call | solution.py:468
  (18 shorter events, 2.3 us)
Async XLA Ops:
  1.5 8.9 %collective-permute-start = (bf16[16,640]{1,0:T(8,128)(2,1)S(1)}, bf16[16,640]{1,0:T(8,128)(2,1)S(1)}, u32[]{:S(2)}, u32[]{:S(2)}) collective-permute-start(bf16[16,640]{1,0:T(8,128)(2,1)S(1)} %get-tuple-element.54), channel_id=1, source_target_pairs={{0,4},{4,8},{8,12},{12,16},{16,20},{20,24},{24,28},{28,32},{32,36}... | collective-permute-start | bytes 61448 | tf_op jit(solution)/shard_map/ppermute | solution.py:506
  11.0 1.7 %collective-permute-start.1 = (bf16[1312,128]{1,0:T(8,128)(2,1)S(1)}, bf16[1312,128]{1,0:T(8,128)(2,1)S(1)}, u32[]{:S(2)}, u32[]{:S(2)}) collective-permute-start(bf16[1312,128]{1,0:T(8,128)(2,1)S(1)} %get-tuple-element.71), channel_id=1, source_target_pairs={{0,4},{4,0},{8,12},{12,8},{16,20},{20,16},{24,28},{28,24},{32,36},... | collective-permute-start | bytes 1007624 | tf_op jit(solution)/shard_map/ppermute | solution.py:526
  12.9 7.0 %collective-permute-start.2 = (bf16[528,128]{1,0:T(8,128)(2,1)S(1)}, bf16[528,128]{1,0:T(8,128)(2,1)S(1)}, u32[]{:S(2)}, u32[]{:S(2)}) collective-permute-start(bf16[528,128]{1,0:T(8,128)(2,1)S(1)} %get-tuple-element.72), channel_id=1, source_target_pairs={{0,8},{4,28},{8,0},{12,20},{16,24},{20,12},{24,16},{28,4},{32,40},... | collective-permute-start | bytes 405512 | tf_op jit(solution)/shard_map/ppermute | solution.py:535
  13.0 8.4 %collective-permute-start.4 = (bf16[272,128]{1,0:T(8,128)(2,1)S(1)}, bf16[272,128]{1,0:T(8,128)(2,1)S(1)}, u32[]{:S(2)}, u32[]{:S(2)}) collective-permute-start(bf16[272,128]{1,0:T(8,128)(2,1)S(1)} %get-tuple-element.81), channel_id=1, source_target_pairs={{0,16},{4,20},{8,24},{12,28},{16,0},{20,4},{24,8},{28,12},{32,48},... | collective-permute-start | bytes 208904 | tf_op jit(solution)/shard_map/ppermute | solution.py:534
  19.9 2.8 %collective-permute-start.3 = (bf16[528,128]{1,0:T(8,128)(2,1)S(1)}, bf16[528,128]{1,0:T(8,128)(2,1)S(1)}, u32[]{:S(2)}, u32[]{:S(2)}) collective-permute-start(bf16[528,128]{1,0:T(8,128)(2,1)S(1)} %collective-permute-done.2.ra_ref), channel_id=1, source_target_pairs={{0,4},{4,0},{8,12},{12,8},{16,20},{20,16},{24,28},{28,24},{32,36},... | collective-permute-start | bytes 405512 | tf_op jit(solution)/shard_map/ppermute | solution.py:550
  21.4 1.3 %collective-permute-start.5 = (bf16[272,128]{1,0:T(8,128)(2,1)S(1)}, bf16[272,128]{1,0:T(8,128)(2,1)S(1)}, u32[]{:S(2)}, u32[]{:S(2)}) collective-permute-start(bf16[272,128]{1,0:T(8,128)(2,1)S(1)} %collective-permute-done.4.rb_ref), channel_id=1, source_target_pairs={{0,4},{4,0},{8,12},{12,8},{16,20},{20,16},{24,28},{28,24},{32,36},... | collective-permute-start | bytes 208904 | tf_op jit(solution)/shard_map/ppermute | solution.py:551
  22.9 9.9 %collective-permute-start.6 = (bf16[528,128]{1,0:T(8,128)(2,1)S(1)}, bf16[528,128]{1,0:T(8,128)(2,1)S(1)}, u32[]{:S(2)}, u32[]{:S(2)}) collective-permute-start(bf16[528,128]{1,0:T(8,128)(2,1)S(1)} %get-tuple-element.82), channel_id=1, source_target_pairs={{0,48},{4,68},{8,56},{12,76},{16,32},{20,84},{24,40},{28,92},{32,8... | collective-permute-start | bytes 405512 | tf_op jit(solution)/shard_map/ppermute | solution.py:557
  27.3 5.5 %collective-permute-start.8 = (bf16[768,128]{1,0:T(8,128)(2,1)S(1)}, bf16[768,128]{1,0:T(8,128)(2,1)S(1)}, u32[]{:S(2)}, u32[]{:S(2)}) collective-permute-start(bf16[768,128]{1,0:T(8,128)(2,1)S(1)} %get-tuple-element.85), channel_id=1, source_target_pairs={{0,4},{4,0},{8,12},{12,8},{16,20},{20,16},{24,28},{28,24},{32,36},... | collective-permute-start | bytes 589832 | tf_op jit(solution)/shard_map/ppermute | solution.py:559
  32.8 1.4 %collective-permute-start.7 = (bf16[528,128]{1,0:T(8,128)(2,1)S(1)}, bf16[528,128]{1,0:T(8,128)(2,1)S(1)}, u32[]{:S(2)}, u32[]{:S(2)}) collective-permute-start(bf16[528,128]{1,0:T(8,128)(2,1)S(1)} %collective-permute-done.6.q_ref), channel_id=1, source_target_pairs={{0,4},{4,0},{8,12},{12,8},{16,20},{20,16},{24,28},{28,24},{32,36},... | collective-permute-start | bytes 405512 | tf_op jit(solution)/shard_map/ppermute | solution.py:560
  34.4 6.9 %collective-permute-start.9 = (bf16[512,128]{1,0:T(8,128)(2,1)S(1)}, bf16[512,128]{1,0:T(8,128)(2,1)S(1)}, u32[]{:S(2)}, u32[]{:S(2)}) collective-permute-start(bf16[512,128]{1,0:T(8,128)(2,1)S(1)} %get-tuple-element.91), channel_id=1, source_target_pairs={{0,8},{4,28},{8,0},{12,20},{16,24},{20,12},{24,16},{28,4},{32,40},... | collective-permute-start | bytes 393224 | tf_op jit(solution)/shard_map/ppermute | solution.py:569
  34.5 8.3 %collective-permute-start.10 = (bf16[256,128]{1,0:T(8,128)(2,1)S(1)}, bf16[256,128]{1,0:T(8,128)(2,1)S(1)}, u32[]{:S(2)}, u32[]{:S(2)}) collective-permute-start(bf16[256,128]{1,0:T(8,128)(2,1)S(1)} %get-tuple-element.92), channel_id=1, source_target_pairs={{0,16},{4,20},{8,24},{12,28},{16,0},{20,4},{24,8},{28,12},{32,48},... | collective-permute-start | bytes 196616 | tf_op jit(solution)/shard_map/ppermute | solution.py:568
  41.3 2.7 %collective-permute-start.11 = (bf16[512,128]{1,0:T(8,128)(2,1)S(1)}, bf16[512,128]{1,0:T(8,128)(2,1)S(1)}, u32[]{:S(2)}, u32[]{:S(2)}) collective-permute-start(bf16[512,128]{1,0:T(8,128)(2,1)S(1)} %collective-permute-done.9.fa_ref), channel_id=1, source_target_pairs={{0,4},{4,0},{8,12},{12,8},{16,20},{20,16},{24,28},{28,24},{32,36},... | collective-permute-start | bytes 393224 | tf_op jit(solution)/shard_map/ppermute | solution.py:570
  42.7 1.3 %collective-permute-start.12 = (bf16[256,128]{1,0:T(8,128)(2,1)S(1)}, bf16[256,128]{1,0:T(8,128)(2,1)S(1)}, u32[]{:S(2)}, u32[]{:S(2)}) collective-permute-start(bf16[256,128]{1,0:T(8,128)(2,1)S(1)} %collective-permute-done.10.fb_ref), channel_id=1, source_target_pairs={{0,4},{4,0},{8,12},{12,8},{16,20},{20,16},{24,28},{28,24},{32,36},... | collective-permute-start | bytes 196616 | tf_op jit(solution)/shard_map/ppermute | solution.py:571
  44.5 5.2 %collective-permute-start.15 = (f32[8,256]{1,0:T(8,128)S(1)}, f32[8,256]{1,0:T(8,128)S(1)}, u32[]{:S(2)}, u32[]{:S(2)}) collective-permute-start(f32[8,256]{1,0:T(8,128)S(1)} %get-tuple-element.100.s0), channel_id=1, source_target_pairs={{0,2},{1,3},{2,0},{3,1},{4,6},{5,7},{6,4},{7,5},{8,10},{9,11},{10,... | collective-permute-start | bytes 24584 | tf_op jit(solution)/shard_map/ppermute | solution.py:581
  47.8 4.9 %collective-permute-start.14 = (f32[8,256]{1,0:T(8,128)S(1)}, f32[8,256]{1,0:T(8,128)S(1)}, u32[]{:S(2)}, u32[]{:S(2)}) collective-permute-start(f32[8,256]{1,0:T(8,128)S(1)} %get-tuple-element.100.s0), channel_id=1, source_target_pairs={{0,3},{1,2},{2,1},{3,0},{4,7},{5,6},{6,5},{7,4},{8,11},{9,10},{10,... | collective-permute-start | bytes 24584 | tf_op jit(solution)/shard_map/ppermute | solution.py:582
  48.9 3.8 %collective-permute-start.13 = (f32[8,256]{1,0:T(8,128)S(1)}, f32[8,256]{1,0:T(8,128)S(1)}, u32[]{:S(2)}, u32[]{:S(2)}) collective-permute-start(f32[8,256]{1,0:T(8,128)S(1)} %get-tuple-element.100.s0), channel_id=1, source_target_pairs={{0,1},{1,0},{2,3},{3,2},{4,5},{5,4},{6,7},{7,6},{8,9},{9,8},{10,11... | collective-permute-start | bytes 24584 | tf_op jit(solution)/shard_map/ppermute | solution.py:583

commit v4 on v3

--- a/solution.py
+++ b/solution.py
@@ -48,9 +48,7 @@
 def to_later_group(x, z, c):
     if c == 0 and z < 4:
         return (x, z ^ 6, c)
-    if x + 1 == XS:
-        return None
-    return (x + 1, z ^ 6 if c == 0 else z, c)
+    return ((x + 1) % XS, z ^ 6 if c == 0 else z, c)
 
 
 LATER = route(to_later_group)
@@ -327,6 +325,9 @@
     before = jnp.where(second, other, q)
     farther = jnp.where(second, q, other)
     decay = joined_decay(before[QUARTER:])
+    group = lax.div(lax.axis_index("ctx"), 8)
+    before = jnp.where(group >= 1, before, 0.0)
+    farther = jnp.where(group >= 2, farther, 0.0)
     for i in range(4):
         rows = slice(i * HD, (i + 1) * HD)
         state = before[rows] + decay[i : i + 1] * farther[rows]

time: 54.1 us -> 54 us (level)
  the two profiles are of different devices: /device:TPU:6 before, /device:TPU:1 now
where the time goes in v4:
time: 54 us; the launch traced here: 53.8 us
  starting transfers between devices  26.6 us (49%)
  waiting for transfers between devices  17.5 us (32%)
  Pallas kernels  9.42 us (17%)
    pallas_call x10, Pallas kernels, call(): pl.pallas_call(kernel, name=name, out_shape=out, in_specs=[HBM if i in fa...  9.42 us
    ppermute x1, starting transfers between devices, body(): ra = lax.ppermute(ta, 'ctx', APART)  5.64 us
    ppermute x1, starting transfers between devices, body(): rim = lax.ppermute(edge, 'ctx', NEXT)  4.94 us
    ppermute x1, starting transfers between devices, body(): other = lax.ppermute(q, 'ctx', CORE)  3.61 us
    ppermute x1, starting transfers between devices, body(): s2 = lax.ppermute(squares, 'head', HEAD_XOR[2])  3 us
    ppermute x1, waiting for transfers between devices, body(): fb = lax.ppermute(eb, 'ctx', TWO)  2.86 us
    ppermute x1, starting transfers between devices, body(): fa = lax.ppermute(ea, 'ctx', APART)  2.85 us
    ppermute x1, waiting for transfers between devices, body(): fa = lax.ppermute(ea, 'ctx', APART)  2.75 us
  transfers between devices with their start and end apart: 16, of which 11 were waited for; matrix products, arithmetic and copies ran while one was open for 0% of the time, Pallas kernels for 9%

profile of v4, /device:TPU:1, one launch (start us, length us, event | category | flops | bytes accessed | tf_op | source)
XLA Modules:
  0.0 53.8 jit_solution(3772772717507782971)
XLA Ops:
  0.0 1.5 %edge.1 = (bf16[16,640]{1,0:T(8,128)(2,1)S(1)}, s32[8,128]{1,0:T(8,128)S(1)}, bf16[256,2048]{1,0:T(8,128)(2,1)S(1)}, bf16[256,256]{1,0:T(8,128)(2,1)S(1)}, f32[4...) custom-call(s32[256]{0:T(256)} %doc_hbm.1, ...), custom_call_target="tpu_custom_call" | custom-call | tf_op jit(solution)/shard_map/edge/pallas_call | solution.py:469
  1.5 4.9 %collective-permute-start = (bf16[16,640]{1,0:T(8,128)(2,1)S(1)}, bf16[16,640]{1,0:T(8,128)(2,1)S(1)}, u32[]{:S(2)}, u32[]{:S(2)}) collective-permute-start(bf16[16,640]{1,0:T(8,128)(2,1)S(1)} %get-tuple-element.54), channel_id=1, source_target_pairs={{0,4},{4,8},{8,12},{12,16},{16,20},{20,24},{24,28},{28,32},{32,36}... | collective-permute-start | bytes 61448 | tf_op jit(solution)/shard_map/ppermute | solution.py:507
  6.4 1.6 %conv.1 = (bf16[256,2048]{1,0:T(8,128)(2,1)S(1)}, bf16[256,256]{1,0:T(8,128)(2,1)S(1)}, f32[16,256]{1,0:T(8,128)S(1)}, f32[16,256]{1,0:T(8,128)S(1)}, f32[16,256]{1,0:T(8,128)S(1)}, /*index=5*/f32[16,128]{1,0:T(8,128)S(1)}) custom-call(s32[8,128]{1,0:T(8,128)S(1)} %get-tuple-element.53.docv_ref, bf16[256,2048]{1,0:T(8,128)(2,1)S(1)} %get-tuple-element.55.feat_ref, ...), custom_call_target="tpu_custom_call" | custom-call | tf_op jit(solution)/shard_map/conv/pallas_call | solution.py:469
  8.0 0.6 %state.1 = (bf16[256,2048]{1,0:T(8,128)(2,1)S(1)}, bf16[256,256]{1,0:T(8,128)(2,1)S(1)}, f32[2048,128]{1,0:T(8,128)S(1)}, bf16[1312,128]{1,0:T(8,128)(2,1)S(1)}, bf16[768,128]{1,0:T(8,128)(2,1)S(1)}) custom-call(s32[8,128]{1,0:T(8,128)S(1)} %get-tuple-element.53.docv_ref, ...), custom_call_target="tpu_custom_call", output_to_operand_aliasing={{0}: (10, {}), {1}: (11, {})} | custom-call | tf_op jit(solution)/shard_map/state/pallas_call | solution.py:469
  8.7 1.6 %collective-permute-done.1.recv_ref = bf16[1312,128]{1,0:T(8,128)(2,1)S(1)} collective-permute-done((bf16[1312,128]{1,0:T(8,128)(2,1)S(1)}, bf16[1312,128]{1,0:T(8,128)(2,1)S(1)}, u32[]{:S(2)}, u32[]{:S(2)}) %collective-permute-start.1) | collective-permute-done | bytes 335904 | tf_op jit(solution)/shard_map/ppermute | solution.py:527
  10.5 5.6 %collective-permute-start.2 = (bf16[528,128]{1,0:T(8,128)(2,1)S(1)}, bf16[528,128]{1,0:T(8,128)(2,1)S(1)}, u32[]{:S(2)}, u32[]{:S(2)}) collective-permute-start(bf16[528,128]{1,0:T(8,128)(2,1)S(1)} %get-tuple-element.72), channel_id=1, source_target_pairs={{0,8},{4,28},{8,0},{12,20},{16,24},{20,12},{24,16},{28,4},{32,40},... | collective-permute-start | bytes 405512 | tf_op jit(solution)/shard_map/ppermute | solution.py:536
  16.2 2.9 %inner.1 = (f32[16,256,128]{2,1,0:T(8,128)S(1)}, f32[16,256,128]{2,1,0:T(8,128)S(1)}, f32[1,2048]{1,0:T(1,128)S(1)}) custom-call(s32[8,128]{1,0:T(8,128)S(1)} %get-tuple-element.53.docv_ref, bf16[256,2048]{1,0:T(8,128)(2,1)S(1)} %get-tuple-element.76.featc_ref, bf16[256,256]{1,0:T(8,128)(2,1)S(1)} %get-tuple-element.73.projc_ref, ...), custom_call_target="tpu_custom_call" | custom-call | tf_op jit(solution)/shard_map/inner/pallas_call | solution.py:469
  19.1 0.6 %collective-permute-done.2.ra_ref = bf16[528,128]{1,0:T(8,128)(2,1)S(1)} collective-permute-done((bf16[528,128]{1,0:T(8,128)(2,1)S(1)}, bf16[528,128]{1,0:T(8,128)(2,1)S(1)}, u32[]{:S(2)}, u32[]{:S(2)}) %collective-permute-start.2) | collective-permute-done | bytes 135200 | tf_op jit(solution)/shard_map/ppermute | solution.py:536
  20.1 1.7 %collective-permute-done.4.rb_ref = bf16[272,128]{1,0:T(8,128)(2,1)S(1)} collective-permute-done((bf16[272,128]{1,0:T(8,128)(2,1)S(1)}, bf16[272,128]{1,0:T(8,128)(2,1)S(1)}, u32[]{:S(2)}, u32[]{:S(2)}) %collective-permute-start.4) | collective-permute-done | bytes 69664 | tf_op jit(solution)/shard_map/ppermute | solution.py:535
  21.8 1.3 %collective-permute-done.5.gb_ref = bf16[272,128]{1,0:T(8,128)(2,1)S(1)} collective-permute-done((bf16[272,128]{1,0:T(8,128)(2,1)S(1)}, bf16[272,128]{1,0:T(8,128)(2,1)S(1)}, u32[]{:S(2)}, u32[]{:S(2)}) %collective-permute-start.5) | collective-permute-done | bytes 69664 | tf_op jit(solution)/shard_map/ppermute | solution.py:552
  23.2 2.0 %collective-permute-start.6 = (bf16[528,128]{1,0:T(8,128)(2,1)S(1)}, bf16[528,128]{1,0:T(8,128)(2,1)S(1)}, u32[]{:S(2)}, u32[]{:S(2)}) collective-permute-start(bf16[528,128]{1,0:T(8,128)(2,1)S(1)} %get-tuple-element.82), channel_id=1, source_target_pairs={{0,48},{4,68},{8,56},{12,76},{16,32},{20,84},{24,40},{28,92},{32,8... | collective-permute-start | bytes 405512 | tf_op jit(solution)/shard_map/ppermute | solution.py:558
  25.2 1.7 %collective-permute-start.8 = (bf16[768,128]{1,0:T(8,128)(2,1)S(1)}, bf16[768,128]{1,0:T(8,128)(2,1)S(1)}, u32[]{:S(2)}, u32[]{:S(2)}) collective-permute-start(bf16[768,128]{1,0:T(8,128)(2,1)S(1)} %get-tuple-element.85), channel_id=1, source_target_pairs={{0,4},{4,0},{8,12},{12,8},{16,20},{20,16},{24,28},{28,24},{32,36},... | collective-permute-start | bytes 589832 | tf_op jit(solution)/shard_map/ppermute | solution.py:560
  27.0 2.3 %collective-permute-done.6.q_ref = bf16[528,128]{1,0:T(8,128)(2,1)S(1)} collective-permute-done((bf16[528,128]{1,0:T(8,128)(2,1)S(1)}, bf16[528,128]{1,0:T(8,128)(2,1)S(1)}, u32[]{:S(2)}, u32[]{:S(2)}) %collective-permute-start.6) | collective-permute-done | bytes 135200 | tf_op jit(solution)/shard_map/ppermute | solution.py:558
  29.2 3.6 %collective-permute-start.7 = (bf16[528,128]{1,0:T(8,128)(2,1)S(1)}, bf16[528,128]{1,0:T(8,128)(2,1)S(1)}, u32[]{:S(2)}, u32[]{:S(2)}) collective-permute-start(bf16[528,128]{1,0:T(8,128)(2,1)S(1)} %collective-permute-done.6.q_ref), channel_id=1, source_target_pairs={{0,4},{4,0},{8,12},{12,8},{16,20},{20,16},{24,28},{28,24},{32,36},... | collective-permute-start | bytes 405512 | tf_op jit(solution)/shard_map/ppermute | solution.py:561
  32.8 1.0 %collective-permute-done.7.other_ref = bf16[528,128]{1,0:T(8,128)(2,1)S(1)} collective-permute-done((bf16[528,128]{1,0:T(8,128)(2,1)S(1)}, bf16[528,128]{1,0:T(8,128)(2,1)S(1)}, u32[]{:S(2)}, u32[]{:S(2)}) %collective-permute-start.7) | collective-permute-done | bytes 135200 | tf_op jit(solution)/shard_map/ppermute | solution.py:561
  34.0 2.8 %collective-permute-start.9 = (bf16[512,128]{1,0:T(8,128)(2,1)S(1)}, bf16[512,128]{1,0:T(8,128)(2,1)S(1)}, u32[]{:S(2)}, u32[]{:S(2)}) collective-permute-start(bf16[512,128]{1,0:T(8,128)(2,1)S(1)} %get-tuple-element.91), channel_id=1, source_target_pairs={{0,8},{4,28},{8,0},{12,20},{16,24},{20,12},{24,16},{28,4},{32,40},... | collective-permute-start | bytes 393224 | tf_op jit(solution)/shard_map/ppermute | solution.py:570
  37.5 2.8 %collective-permute-done.9.fa_ref = bf16[512,128]{1,0:T(8,128)(2,1)S(1)} collective-permute-done((bf16[512,128]{1,0:T(8,128)(2,1)S(1)}, bf16[512,128]{1,0:T(8,128)(2,1)S(1)}, u32[]{:S(2)}, u32[]{:S(2)}) %collective-permute-start.9) | collective-permute-done | bytes 131104 | tf_op jit(solution)/shard_map/ppermute | solution.py:570
  40.2 0.9 %collective-permute-start.11 = (bf16[512,128]{1,0:T(8,128)(2,1)S(1)}, bf16[512,128]{1,0:T(8,128)(2,1)S(1)}, u32[]{:S(2)}, u32[]{:S(2)}) collective-permute-start(bf16[512,128]{1,0:T(8,128)(2,1)S(1)} %collective-permute-done.9.fa_ref), channel_id=1, source_target_pairs={{0,4},{4,0},{8,12},{12,8},{16,20},{20,16},{24,28},{28,24},{32,36},... | collective-permute-start | bytes 393224 | tf_op jit(solution)/shard_map/ppermute | solution.py:571
  41.1 2.9 %collective-permute-done.10.fb_ref = bf16[256,128]{1,0:T(8,128)(2,1)S(1)} collective-permute-done((bf16[256,128]{1,0:T(8,128)(2,1)S(1)}, bf16[256,128]{1,0:T(8,128)(2,1)S(1)}, u32[]{:S(2)}, u32[]{:S(2)}) %collective-permute-start.10) | collective-permute-done | bytes 65568 | tf_op jit(solution)/shard_map/ppermute | solution.py:569
  44.0 0.6 %gated.1 = (f32[16,256,128]{2,1,0:T(8,128)S(1)}, f32[256,128]{1,0:T(8,128)S(1)}, f32[16,128]{1,0:T(8,128)S(1)}) custom-call(bf16[256,256]{1,0:T(8,128)(2,1)S(1)} %get-tuple-element.73.projc_ref, bf16[1312,128]{1,0:T(8,128)(2,1)S(1)} %collective-permute-done.1.recv_ref, f32[512,128]{1,0:T(8,128)S(1)} %get-tuple-element.90.own_ref, ...), custom_call_target="tpu_custom_call" | custom-call | tf_op jit(solution)/shard_map/gated/pallas_call | solution.py:469
  45.7 3.0 %collective-permute-start.15 = (f32[8,256]{1,0:T(8,128)S(1)}, f32[8,256]{1,0:T(8,128)S(1)}, u32[]{:S(2)}, u32[]{:S(2)}) collective-permute-start(f32[8,256]{1,0:T(8,128)S(1)} %get-tuple-element.100.s0), channel_id=1, source_target_pairs={{0,2},{1,3},{2,0},{3,1},{4,6},{5,7},{6,4},{7,5},{8,10},{9,11},{10,... | collective-permute-start | bytes 24584 | tf_op jit(solution)/shard_map/ppermute | solution.py:582
  48.7 0.8 %collective-permute-start.14 = (f32[8,256]{1,0:T(8,128)S(1)}, f32[8,256]{1,0:T(8,128)S(1)}, u32[]{:S(2)}, u32[]{:S(2)}) collective-permute-start(f32[8,256]{1,0:T(8,128)S(1)} %get-tuple-element.100.s0), channel_id=1, source_target_pairs={{0,3},{1,2},{2,1},{3,0},{4,7},{5,6},{6,5},{7,4},{8,11},{9,10},{10,... | collective-permute-start | bytes 24584 | tf_op jit(solution)/shard_map/ppermute | solution.py:583
  49.8 2.6 %collective-permute-done.14.s3 = f32[8,256]{1,0:T(8,128)S(1)} collective-permute-done((f32[8,256]{1,0:T(8,128)S(1)}, f32[8,256]{1,0:T(8,128)S(1)}, u32[]{:S(2)}, u32[]{:S(2)}) %collective-permute-start.14) | collective-permute-done | bytes 8224 | tf_op jit(solution)/shard_map/ppermute | solution.py:583
  52.4 1.3 %norm.1 = bf16[256,2048]{1,0:T(8,128)(2,1)} custom-call(f32[16,256,128]{2,1,0:T(8,128)S(1)} %get-tuple-element.99.gated_ref, f32[8,256]{1,0:T(8,128)S(1)} %get-tuple-element.100.s0, f32[8,256]{1,0:T(8,128)S(1)} %collective-permute-done.13.s1, f32[8,256]{1,0:T(8,128)S(1)} %collective-permute-done.14.s3, f32[8,256]{1,0:T(8,128)S(1)} %collective-permute-done.15.s2), custom_call_target="tpu_custom_call" | custom-call | tf_op jit(solution)/shard_map/norm/pallas_call | solution.py:469
  (18 shorter events, 3.2 us)
Async XLA Ops:
  1.5 6.5 %collective-permute-start = (bf16[16,640]{1,0:T(8,128)(2,1)S(1)}, bf16[16,640]{1,0:T(8,128)(2,1)S(1)}, u32[]{:S(2)}, u32[]{:S(2)}) collective-permute-start(bf16[16,640]{1,0:T(8,128)(2,1)S(1)} %get-tuple-element.54), channel_id=1, source_target_pairs={{0,4},{4,8},{8,12},{12,16},{16,20},{20,24},{24,28},{28,32},{32,36}... | collective-permute-start | bytes 61448 | tf_op jit(solution)/shard_map/ppermute | solution.py:507
  8.6 1.7 %collective-permute-start.1 = (bf16[1312,128]{1,0:T(8,128)(2,1)S(1)}, bf16[1312,128]{1,0:T(8,128)(2,1)S(1)}, u32[]{:S(2)}, u32[]{:S(2)}) collective-permute-start(bf16[1312,128]{1,0:T(8,128)(2,1)S(1)} %get-tuple-element.71), channel_id=1, source_target_pairs={{0,4},{4,0},{8,12},{12,8},{16,20},{20,16},{24,28},{28,24},{32,36},... | collective-permute-start | bytes 1007624 | tf_op jit(solution)/shard_map/ppermute | solution.py:527
  10.5 9.2 %collective-permute-start.2 = (bf16[528,128]{1,0:T(8,128)(2,1)S(1)}, bf16[528,128]{1,0:T(8,128)(2,1)S(1)}, u32[]{:S(2)}, u32[]{:S(2)}) collective-permute-start(bf16[528,128]{1,0:T(8,128)(2,1)S(1)} %get-tuple-element.72), channel_id=1, source_target_pairs={{0,8},{4,28},{8,0},{12,20},{16,24},{20,12},{24,16},{28,4},{32,40},... | collective-permute-start | bytes 405512 | tf_op jit(solution)/shard_map/ppermute | solution.py:536
  16.2 5.7 %collective-permute-start.4 = (bf16[272,128]{1,0:T(8,128)(2,1)S(1)}, bf16[272,128]{1,0:T(8,128)(2,1)S(1)}, u32[]{:S(2)}, u32[]{:S(2)}) collective-permute-start(bf16[272,128]{1,0:T(8,128)(2,1)S(1)} %get-tuple-element.81), channel_id=1, source_target_pairs={{0,16},{4,20},{8,24},{12,28},{16,0},{20,4},{24,8},{28,12},{32,48},... | collective-permute-start | bytes 208904 | tf_op jit(solution)/shard_map/ppermute | solution.py:535
  19.7 3.4 %collective-permute-start.3 = (bf16[528,128]{1,0:T(8,128)(2,1)S(1)}, bf16[528,128]{1,0:T(8,128)(2,1)S(1)}, u32[]{:S(2)}, u32[]{:S(2)}) collective-permute-start(bf16[528,128]{1,0:T(8,128)(2,1)S(1)} %collective-permute-done.2.ra_ref), channel_id=1, source_target_pairs={{0,4},{4,0},{8,12},{12,8},{16,20},{20,16},{24,28},{28,24},{32,36},... | collective-permute-start | bytes 405512 | tf_op jit(solution)/shard_map/ppermute | solution.py:551
  21.8 1.3 %collective-permute-start.5 = (bf16[272,128]{1,0:T(8,128)(2,1)S(1)}, bf16[272,128]{1,0:T(8,128)(2,1)S(1)}, u32[]{:S(2)}, u32[]{:S(2)}) collective-permute-start(bf16[272,128]{1,0:T(8,128)(2,1)S(1)} %collective-permute-done.4.rb_ref), channel_id=1, source_target_pairs={{0,4},{4,0},{8,12},{12,8},{16,20},{20,16},{24,28},{28,24},{32,36},... | collective-permute-start | bytes 208904 | tf_op jit(solution)/shard_map/ppermute | solution.py:552
  23.2 6.0 %collective-permute-start.6 = (bf16[528,128]{1,0:T(8,128)(2,1)S(1)}, bf16[528,128]{1,0:T(8,128)(2,1)S(1)}, u32[]{:S(2)}, u32[]{:S(2)}) collective-permute-start(bf16[528,128]{1,0:T(8,128)(2,1)S(1)} %get-tuple-element.82), channel_id=1, source_target_pairs={{0,48},{4,68},{8,56},{12,76},{16,32},{20,84},{24,40},{28,92},{32,8... | collective-permute-start | bytes 405512 | tf_op jit(solution)/shard_map/ppermute | solution.py:558
  25.2 7.6 %collective-permute-start.8 = (bf16[768,128]{1,0:T(8,128)(2,1)S(1)}, bf16[768,128]{1,0:T(8,128)(2,1)S(1)}, u32[]{:S(2)}, u32[]{:S(2)}) collective-permute-start(bf16[768,128]{1,0:T(8,128)(2,1)S(1)} %get-tuple-element.85), channel_id=1, source_target_pairs={{0,4},{4,0},{8,12},{12,8},{16,20},{20,16},{24,28},{28,24},{32,36},... | collective-permute-start | bytes 589832 | tf_op jit(solution)/shard_map/ppermute | solution.py:560
  29.2 4.6 %collective-permute-start.7 = (bf16[528,128]{1,0:T(8,128)(2,1)S(1)}, bf16[528,128]{1,0:T(8,128)(2,1)S(1)}, u32[]{:S(2)}, u32[]{:S(2)}) collective-permute-start(bf16[528,128]{1,0:T(8,128)(2,1)S(1)} %collective-permute-done.6.q_ref), channel_id=1, source_target_pairs={{0,4},{4,0},{8,12},{12,8},{16,20},{20,16},{24,28},{28,24},{32,36},... | collective-permute-start | bytes 405512 | tf_op jit(solution)/shard_map/ppermute | solution.py:561
  34.0 6.2 %collective-permute-start.9 = (bf16[512,128]{1,0:T(8,128)(2,1)S(1)}, bf16[512,128]{1,0:T(8,128)(2,1)S(1)}, u32[]{:S(2)}, u32[]{:S(2)}) collective-permute-start(bf16[512,128]{1,0:T(8,128)(2,1)S(1)} %get-tuple-element.91), channel_id=1, source_target_pairs={{0,8},{4,28},{8,0},{12,20},{16,24},{20,12},{24,16},{28,4},{32,40},... | collective-permute-start | bytes 393224 | tf_op jit(solution)/shard_map/ppermute | solution.py:570
  36.9 7.0 %collective-permute-start.10 = (bf16[256,128]{1,0:T(8,128)(2,1)S(1)}, bf16[256,128]{1,0:T(8,128)(2,1)S(1)}, u32[]{:S(2)}, u32[]{:S(2)}) collective-permute-start(bf16[256,128]{1,0:T(8,128)(2,1)S(1)} %get-tuple-element.92), channel_id=1, source_target_pairs={{0,16},{4,20},{8,24},{12,28},{16,0},{20,4},{24,8},{28,12},{32,48},... | collective-permute-start | bytes 196616 | tf_op jit(solution)/shard_map/ppermute | solution.py:569
  40.2 5.0 %collective-permute-start.11 = (bf16[512,128]{1,0:T(8,128)(2,1)S(1)}, bf16[512,128]{1,0:T(8,128)(2,1)S(1)}, u32[]{:S(2)}, u32[]{:S(2)}) collective-permute-start(bf16[512,128]{1,0:T(8,128)(2,1)S(1)} %collective-permute-done.9.fa_ref), channel_id=1, source_target_pairs={{0,4},{4,0},{8,12},{12,8},{16,20},{20,16},{24,28},{28,24},{32,36},... | collective-permute-start | bytes 393224 | tf_op jit(solution)/shard_map/ppermute | solution.py:571
  43.9 1.3 %collective-permute-start.12 = (bf16[256,128]{1,0:T(8,128)(2,1)S(1)}, bf16[256,128]{1,0:T(8,128)(2,1)S(1)}, u32[]{:S(2)}, u32[]{:S(2)}) collective-permute-start(bf16[256,128]{1,0:T(8,128)(2,1)S(1)} %collective-permute-done.10.fb_ref), channel_id=1, source_target_pairs={{0,4},{4,0},{8,12},{12,8},{16,20},{20,16},{24,28},{28,24},{32,36},... | collective-permute-start | bytes 196616 | tf_op jit(solution)/shard_map/ppermute | solution.py:572
  45.7 4.1 %collective-permute-start.15 = (f32[8,256]{1,0:T(8,128)S(1)}, f32[8,256]{1,0:T(8,128)S(1)}, u32[]{:S(2)}, u32[]{:S(2)}) collective-permute-start(f32[8,256]{1,0:T(8,128)S(1)} %get-tuple-element.100.s0), channel_id=1, source_target_pairs={{0,2},{1,3},{2,0},{3,1},{4,6},{5,7},{6,4},{7,5},{8,10},{9,11},{10,... | collective-permute-start | bytes 24584 | tf_op jit(solution)/shard_map/ppermute | solution.py:582
  48.7 3.7 %collective-permute-start.14 = (f32[8,256]{1,0:T(8,128)S(1)}, f32[8,256]{1,0:T(8,128)S(1)}, u32[]{:S(2)}, u32[]{:S(2)}) collective-permute-start(f32[8,256]{1,0:T(8,128)S(1)} %get-tuple-element.100.s0), channel_id=1, source_target_pairs={{0,3},{1,2},{2,1},{3,0},{4,7},{5,6},{6,5},{7,4},{8,11},{9,10},{10,... | collective-permute-start | bytes 24584 | tf_op jit(solution)/shard_map/ppermute | solution.py:583
  49.5 2.9 %collective-permute-start.13 = (f32[8,256]{1,0:T(8,128)S(1)}, f32[8,256]{1,0:T(8,128)S(1)}, u32[]{:S(2)}, u32[]{:S(2)}) collective-permute-start(f32[8,256]{1,0:T(8,128)S(1)} %get-tuple-element.100.s0), channel_id=1, source_target_pairs={{0,1},{1,0},{2,3},{3,2},{4,5},{5,4},{6,7},{7,6},{8,9},{9,8},{10,11... | collective-permute-start | bytes 24584 | tf_op jit(solution)/shard_map/ppermute | solution.py:584
